TPU v7x, 512 devices: a whole 4x4x16 slice. The times are simulated.
512 devices in a mesh: ctx: 64 (over z, y_hi, core), head: 8 (over y_lo, x).
Axes of the slice: x: 4, y: 4 (y_hi: 2, y_lo: 2; y = y_hi * 2 + y_lo), z: 16, core: 2. Of those that a mesh axis runs over, the one named last changes fastest.
Arguments:
- query: bfloat16 [8192, 128, 128], P(('ctx', 'head')), may hold values from -6 to 6
- key: bfloat16 [8192, 8, 128], P(('ctx', 'head')), may hold values from -6 to 6
- value: bfloat16 [8192, 8, 128], P(('ctx', 'head')), may hold values from -6 to 6
- out_grad: bfloat16 [8192, 128, 128], P(('ctx', 'head')), may hold values from -6 to 6
- doc_lengths: int32 [16], replicated, may hold values from 1 to 1024, 8192 in all
Outputs:
- attended: bfloat16 [8192, 128, 128], P(('ctx', 'head'))
- query_grad: bfloat16 [8192, 128, 128], P(('ctx', 'head'))
- key_grad: bfloat16 [8192, 8, 128], P(('ctx', 'head'))
- value_grad: bfloat16 [8192, 8, 128], P(('ctx', 'head'))
Inputs may be any that keep to these rules, and one draw needn't show every extreme that they name: `doc_lengths`: they sum to 8192; the longest is 1024.
All inputs are finite; a program needn't handle non-finite values.
Results may differ from a plain program's by a relative error of at most 0.039.
Values may be sent and summed in bfloat16 or wider, within the bound.
No kernel may reach another device: no remote copies, remote signals or barrier semaphores. Data moves between devices by JAX's collectives and lax.ppermute only.
A program may use at most 64 MiB of HBM per device.

v0:
```python
import jax
import jax.numpy as jnp
from jax import lax
from jax.sharding import PartitionSpec as P

REACH = 8


NEGATIVE = -1e30


def shifted(block, axis, distance):
    devices = range(lax.axis_size(axis))
    route = [(i - distance, i) for i in devices if i - distance in devices]
    return lax.ppermute(block, axis, route)


def doc_starts(doc_lengths, position):
    ends = jnp.cumsum(doc_lengths)
    begins = ends - doc_lengths
    inside = begins[None, :] <= position[:, None]
    return jnp.max(jnp.where(inside, begins[None, :], 0), axis=1)


def on_device(query, key, value, out_grad, doc_lengths):
    query_here, key_here, value_here, grad_here = (
        lax.all_to_all(query, "head", split_axis=1, concat_axis=0, tiled=True),
        lax.all_to_all(key, "head", split_axis=1, concat_axis=0, tiled=True),
        lax.all_to_all(value, "head", split_axis=1, concat_axis=0, tiled=True),
        lax.all_to_all(out_grad, "head", split_axis=1, concat_axis=0, tiled=True),
    )
    tok_rows, local_heads, head_width = query_here.shape
    local_kv = key_here.shape[1]
    group_size = local_heads // local_kv
    inv_root = head_width ** (-0.5)
    grouped = query_here.reshape(tok_rows, local_kv, group_size, head_width)
    ctx_place = lax.axis_index("ctx")
    row_range = jnp.arange(tok_rows, dtype=jnp.int32)
    query_pos = ctx_place * tok_rows + row_range
    doc_start = doc_starts(doc_lengths, query_pos)
    own_pair = jnp.stack([key_here, value_here])
    blocks = [own_pair]
    moving = own_pair
    for distance in range(REACH):
        moving = shifted(moving, "ctx", 1)
        blocks.append(moving)
    masks = []
    lively = []
    for distance in range(REACH + 1):
        key_pos = (ctx_place - distance) * tok_rows + row_range
        masks.append(
            (key_pos[None, :] >= doc_start[:, None]) & (key_pos[None, :] <= query_pos[:, None])
        )
        lively.append(
            (ctx_place >= distance)
            & ((ctx_place - distance) * tok_rows + tok_rows - 1 >= doc_start[0])
        )

    def block_scores(pair, allowed):
        raw = (
            jnp.einsum("tkgd,skd->kgts", grouped, pair[0], preferred_element_type=jnp.float32)
            * inv_root
        )
        return jnp.where(allowed, raw, NEGATIVE)

    first_scores = block_scores(blocks[0], masks[0])
    running = jnp.max(first_scores, axis=-1)
    totals = jnp.sum(jnp.exp(first_scores - running[..., None]), axis=-1)
    for distance in range(1, REACH + 1):

        def grow(state, pair=blocks[distance], allowed=masks[distance]):
            running_old, totals_old = state
            scores = block_scores(pair, allowed)
            running_new = jnp.maximum(running_old, jnp.max(scores, axis=-1))
            totals_new = totals_old * jnp.exp(running_old - running_new)
            totals_new = totals_new + jnp.sum(jnp.exp(scores - running_new[..., None]), axis=-1)
            return (running_new, totals_new)

        running, totals = grow((running, totals))
    log_total = running + jnp.log(totals)
    out_acc = jnp.zeros((tok_rows, local_kv, group_size, head_width), jnp.float32)
    prob_list = []
    for distance in range(REACH + 1):

        def forward_tile(acc_in, pair=blocks[distance], allowed=masks[distance]):
            scores = block_scores(pair, allowed)
            weights = jnp.where(allowed, jnp.exp(scores - log_total[..., None]), 0.0).astype(
                jnp.bfloat16
            )
            added = jnp.einsum(
                "kgts,skd->tkgd", weights, pair[1], preferred_element_type=jnp.float32
            )
            return (acc_in + added, weights)

        out_acc, weights = forward_tile(out_acc)
        prob_list.append(weights)
    attended = out_acc.astype(jnp.bfloat16)
    grad_group = grad_here.reshape(tok_rows, local_kv, group_size, head_width)
    row_delta = jnp.transpose(
        jnp.sum(grad_group.astype(jnp.float32) * attended.astype(jnp.float32), axis=-1), (1, 2, 0)
    )
    query_acc = jnp.zeros((tok_rows, local_kv, group_size, head_width), jnp.float32)
    pieces = []
    for distance in range(REACH + 1):

        def backward_tile(acc_in, pair=blocks[distance], weights=prob_list[distance]):
            dprob = jnp.einsum(
                "tkgd,skd->kgts", grad_group, pair[1], preferred_element_type=jnp.float32
            )
            dscore = (
                weights.astype(jnp.float32) * (dprob - row_delta[..., None]) * inv_root
            ).astype(jnp.bfloat16)
            acc_out = acc_in + jnp.einsum(
                "kgts,skd->tkgd", dscore, pair[0], preferred_element_type=jnp.float32
            )
            key_part = jnp.einsum(
                "kgts,tkgd->skd", dscore, grouped, preferred_element_type=jnp.float32
            )
            value_part = jnp.einsum(
                "kgts,tkgd->skd", weights, grad_group, preferred_element_type=jnp.float32
            )
            return (acc_out, jnp.stack([key_part, value_part]))

        query_acc, piece = backward_tile(query_acc)
        pieces.append(piece)
    gathered = pieces[REACH]
    for distance in range(REACH - 1, -1, -1):
        gathered = (
            shifted(gathered.astype(jnp.bfloat16), "ctx", -1).astype(gathered.dtype)
            + pieces[distance]
        )
    key_grad = gathered[0].astype(jnp.bfloat16)
    value_grad = gathered[1].astype(jnp.bfloat16)
    query_grad = query_acc.astype(jnp.bfloat16).reshape(tok_rows, local_heads, head_width)
    attended_flat = attended.reshape(tok_rows, local_heads, head_width)
    return (
        lax.all_to_all(attended_flat, "head", split_axis=0, concat_axis=1, tiled=True),
        lax.all_to_all(query_grad, "head", split_axis=0, concat_axis=1, tiled=True),
        lax.all_to_all(key_grad, "head", split_axis=0, concat_axis=1, tiled=True),
        lax.all_to_all(value_grad, "head", split_axis=0, concat_axis=1, tiled=True),
    )


def solution(mesh):
    placed = (
        P(("ctx", "head"), None, None),
        P(("ctx", "head"), None, None),
        P(("ctx", "head"), None, None),
        P(("ctx", "head"), None, None),
        P(),
    )
    return jax.shard_map(
        on_device,
        mesh=mesh,
        in_specs=placed,
        out_specs=(
            P(("ctx", "head"), None, None),
            P(("ctx", "head"), None, None),
            P(("ctx", "head"), None, None),
            P(("ctx", "head"), None, None),
        ),
        check_vma=False,
    )
```

profile of v0, /device:TPU:256, one launch (start us, length us, event | category | flops | bytes accessed | tf_op | source)
XLA Modules:
  0.0 236.0 jit_solution(4181250230941414602)
XLA Ops:
  2.0 5.4 %all-to-all-start = ((bf16[16,8,128]{2,0,1:T(8,128)(2,1)}), bf16[16,8,128]{2,0,1:T(8,128)(2,1)S(1)}, u32[]{:S(2)}, u32[]{:S(2)}) async-start(bf16[16,8,128]{2,0,1:T(8,128)(2,1)} %copy.297), calls=%async_computation | async-start | bytes 65536 | tf_op jit(solution)/shard_map/all_to_all | solution.py:28
  8.1 5.6 %all-to-all-done = bf16[16,8,128]{2,0,1:T(8,128)(2,1)S(1)} async-done(((bf16[16,8,128]{2,0,1:T(8,128)(2,1)}), bf16[16,8,128]{2,0,1:T(8,128)(2,1)S(1)}, u32[]{:S(2)}, u32[]{:S(2)}) %all-to-all-start) | async-done | bytes 32800 | tf_op jit(solution)/shard_map/all_to_all | solution.py:28
  13.7 3.3 %all-to-all-start.2 = ((bf16[16,8,128]{2,0,1:T(8,128)(2,1)}), bf16[16,8,128]{2,0,1:T(8,128)(2,1)S(1)}, u32[]{:S(2)}, u32[]{:S(2)}) async-start(bf16[16,8,128]{2,0,1:T(8,128)(2,1)} %copy.300), calls=%async_computation.2 | async-start | bytes 65536 | tf_op jit(solution)/shard_map/all_to_all | solution.py:29
  18.0 2.2 copy.298
  20.2 3.1 %all-to-all-done.2 = bf16[16,8,128]{2,0,1:T(8,128)(2,1)S(1)} async-done(((bf16[16,8,128]{2,0,1:T(8,128)(2,1)}), bf16[16,8,128]{2,0,1:T(8,128)(2,1)S(1)}, u32[]{:S(2)}, u32[]{:S(2)}) %all-to-all-start.2) | async-done | bytes 32800 | tf_op jit(solution)/shard_map/all_to_all | solution.py:29
  23.3 3.5 %all-to-all-start.1 = ((bf16[16,128,128]{2,0,1:T(8,128)(2,1)}), bf16[16,128,128]{2,0,1:T(8,128)(2,1)S(1)}, u32[]{:S(2)}, u32[]{:S(2)}) async-start(bf16[16,128,128]{2,0,1:T(8,128)(2,1)} %copy.298), calls=%async_computation.1 | async-start | bytes 1048576 | tf_op jit(solution)/shard_map/all_to_all | solution.py:27
  26.8 1.9 collective-permute-start
  28.8 7.7 %collective-permute-done = bf16[2,128,1,128]{3,1,2,0:T(8,128)(2,1)S(1)} collective-permute-done((bf16[2,128,1,128]{3,1,2,0:T(8,128)(2,1)S(1)}, bf16[2,128,1,128]{3,1,2,0:T(8,128)(2,1)S(1)}, u32[]{:S(2)}, u32[]{:S(2)}) %collective-permute-start) | collective-permute-done | bytes 65568 | tf_op jit(solution)/shard_map/ppermute | solution.py:15
  36.5 1.9 collective-permute-start.1
  38.4 7.3 %collective-permute-done.1 = bf16[2,128,1,128]{3,1,2,0:T(8,128)(2,1)S(1)} collective-permute-done((bf16[2,128,1,128]{3,1,2,0:T(8,128)(2,1)S(1)}, bf16[2,128,1,128]{3,1,2,0:T(8,128)(2,1)S(1)}, u32[]{:S(2)}, u32[]{:S(2)}) %collective-permute-start.1) | collective-permute-done | bytes 65568 | tf_op jit(solution)/shard_map/ppermute | solution.py:15
  45.7 1.9 collective-permute-start.2
  47.6 7.2 %collective-permute-done.2 = bf16[2,128,1,128]{3,1,2,0:T(8,128)(2,1)S(1)} collective-permute-done((bf16[2,128,1,128]{3,1,2,0:T(8,128)(2,1)S(1)}, bf16[2,128,1,128]{3,1,2,0:T(8,128)(2,1)S(1)}, u32[]{:S(2)}, u32[]{:S(2)}) %collective-permute-start.2) | collective-permute-done | bytes 65568 | tf_op jit(solution)/shard_map/ppermute | solution.py:15
  54.9 1.9 collective-permute-start.3
  56.8 7.3 %collective-permute-done.3 = bf16[2,128,1,128]{3,1,2,0:T(8,128)(2,1)S(1)} collective-permute-done((bf16[2,128,1,128]{3,1,2,0:T(8,128)(2,1)S(1)}, bf16[2,128,1,128]{3,1,2,0:T(8,128)(2,1)S(1)}, u32[]{:S(2)}, u32[]{:S(2)}) %collective-permute-start.3) | collective-permute-done | bytes 65568 | tf_op jit(solution)/shard_map/ppermute | solution.py:15
  64.0 1.9 collective-permute-start.4
  66.0 7.3 %collective-permute-done.4 = bf16[2,128,1,128]{3,1,2,0:T(8,128)(2,1)S(1)} collective-permute-done((bf16[2,128,1,128]{3,1,2,0:T(8,128)(2,1)S(1)}, bf16[2,128,1,128]{3,1,2,0:T(8,128)(2,1)S(1)}, u32[]{:S(2)}, u32[]{:S(2)}) %collective-permute-start.4) | collective-permute-done | bytes 65568 | tf_op jit(solution)/shard_map/ppermute | solution.py:15
  73.2 1.9 collective-permute-start.5
  77.1 5.4 %collective-permute-done.5 = bf16[2,128,1,128]{3,1,2,0:T(8,128)(2,1)} collective-permute-done((bf16[2,128,1,128]{3,1,2,0:T(8,128)(2,1)S(1)}, bf16[2,128,1,128]{3,1,2,0:T(8,128)(2,1)}, u32[]{:S(2)}, u32[]{:S(2)}) %collective-permute-start.5) | collective-permute-done | bytes 65568 | tf_op jit(solution)/shard_map/ppermute | solution.py:15
  82.5 1.9 collective-permute-start.6
  84.5 5.1 %all-to-all-start.4 = ((bf16[16,128,128]{2,0,1:T(8,128)(2,1)}), bf16[16,128,128]{2,0,1:T(8,128)(2,1)S(1)}, u32[]{:S(2)}, u32[]{:S(2)}) async-start(bf16[16,128,128]{2,0,1:T(8,128)(2,1)} %copy.321), calls=%async_computation.4 | async-start | bytes 1048576 | tf_op jit(solution)/shard_map/all_to_all | solution.py:30
  90.4 1.7 fusion.99
  92.1 1.9 fusion.100
  93.9 1.9 fusion.101
  95.9 1.9 fusion.102
  97.8 1.9 fusion.103
  99.6 1.9 fusion.105
  104.2 2.5 %copy.325 = f32[128,1,16,128]{0,3,2,1:T(8,128)} copy(f32[128,1,16,128]{3,2,0,1:T(8,128)} %bitcast.731) | data formatting | bytes 2097152 | tf_op jit(solution)/shard_map/convert_element_type | solution.py:100
  107.8 2.1 collective-permute-start.7
  111.1 6.5 %collective-permute-done.7 = bf16[2,128,1,128]{3,1,2,0:T(8,128)(2,1)S(1)} collective-permute-done((bf16[2,128,1,128]{3,1,2,0:T(8,128)(2,1)}, bf16[2,128,1,128]{3,1,2,0:T(8,128)(2,1)S(1)}, u32[]{:S(2)}, u32[]{:S(2)}) %collective-permute-start.7) | collective-permute-done | bytes 65568 | tf_op jit(solution)/shard_map/ppermute | solution.py:15
  123.0 1.7 select_convert_fusion
  131.8 2.1 collective-permute-start.8
  144.1 2.0 collective-permute-start.9
  146.4 1.6 collective-permute-done.9
  148.1 7.3 %collective-permute-start.10 = (bf16[2,128,1,128]{3,1,2,0:T(8,128)(2,1)S(1)}, bf16[2,128,1,128]{3,1,2,0:T(8,128)(2,1)S(1)}, u32[]{:S(2)}, u32[]{:S(2)}) collective-permute-start(bf16[2,128,1,128]{3,1,2,0:T(8,128)(2,1)S(1)} %fusion.89), channel_id=1, source_target_pairs={{8,0},{16,8},{24,16},{32,24},{40,32},{48,40},{56,48},{64,56},{72,6... | collective-permute-start | bytes 196616 | tf_op jit(solution)/shard_map/ppermute | solution.py:15
  155.7 1.6 collective-permute-done.10
  157.3 7.3 %collective-permute-start.11 = (bf16[2,128,1,128]{3,1,2,0:T(8,128)(2,1)S(1)}, bf16[2,128,1,128]{3,1,2,0:T(8,128)(2,1)S(1)}, u32[]{:S(2)}, u32[]{:S(2)}) collective-permute-start(bf16[2,128,1,128]{3,1,2,0:T(8,128)(2,1)S(1)} %fusion.90), channel_id=1, source_target_pairs={{8,0},{16,8},{24,16},{32,24},{40,32},{48,40},{56,48},{64,56},{72,6... | collective-permute-start | bytes 196616 | tf_op jit(solution)/shard_map/ppermute | solution.py:15
  166.5 7.3 %collective-permute-start.12 = (bf16[2,128,1,128]{3,1,2,0:T(8,128)(2,1)S(1)}, bf16[2,128,1,128]{3,1,2,0:T(8,128)(2,1)S(1)}, u32[]{:S(2)}, u32[]{:S(2)}) collective-permute-start(bf16[2,128,1,128]{3,1,2,0:T(8,128)(2,1)S(1)} %fusion.91), channel_id=1, source_target_pairs={{8,0},{16,8},{24,16},{32,24},{40,32},{48,40},{56,48},{64,56},{72,6... | collective-permute-start | bytes 196616 | tf_op jit(solution)/shard_map/ppermute | solution.py:15
  174.1 1.6 collective-permute-done.12
  175.7 7.4 %collective-permute-start.13 = (bf16[2,128,1,128]{3,1,2,0:T(8,128)(2,1)S(1)}, bf16[2,128,1,128]{3,1,2,0:T(8,128)(2,1)S(1)}, u32[]{:S(2)}, u32[]{:S(2)}) collective-permute-start(bf16[2,128,1,128]{3,1,2,0:T(8,128)(2,1)S(1)} %fusion.92), channel_id=1, source_target_pairs={{8,0},{16,8},{24,16},{32,24},{40,32},{48,40},{56,48},{64,56},{72,6... | collective-permute-start | bytes 196616 | tf_op jit(solution)/shard_map/ppermute | solution.py:15
  184.5 5.2 %all-to-all-start.5 = ((bf16[128,16,128]{2,1,0:T(8,128)(2,1)}), bf16[128,16,128]{2,1,0:T(8,128)(2,1)S(1)}, u32[]{:S(2)}, u32[]{:S(2)}) async-start(bf16[128,16,128]{2,1,0:T(8,128)(2,1)} %copy.351), calls=%async_computation.5 | async-start | bytes 1048576 | tf_op jit(solution)/shard_map/all_to_all | solution.py:138
  189.8 2.5 %collective-permute-start.14 = (bf16[2,128,1,128]{3,1,2,0:T(8,128)(2,1)S(1)}, bf16[2,128,1,128]{3,1,2,0:T(8,128)(2,1)S(1)}, u32[]{:S(2)}, u32[]{:S(2)}) collective-permute-start(bf16[2,128,1,128]{3,1,2,0:T(8,128)(2,1)S(1)} %fusion.93), channel_id=1, source_target_pairs={{8,0},{16,8},{24,16},{32,24},{40,32},{48,40},{56,48},{64,56},{72,6... | collective-permute-start | bytes 196616 | tf_op jit(solution)/shard_map/ppermute | solution.py:15
  194.2 7.9 %collective-permute-start.15 = (bf16[2,128,1,128]{3,1,2,0:T(8,128)(2,1)S(1)}, bf16[2,128,1,128]{3,1,2,0:T(8,128)(2,1)S(1)}, u32[]{:S(2)}, u32[]{:S(2)}) collective-permute-start(bf16[2,128,1,128]{3,1,2,0:T(8,128)(2,1)S(1)} %fusion.94), channel_id=1, source_target_pairs={{8,0},{16,8},{24,16},{32,24},{40,32},{48,40},{56,48},{64,56},{72,6... | collective-permute-start | bytes 196616 | tf_op jit(solution)/shard_map/ppermute | solution.py:15
  202.1 5.5 %all-to-all-start.3 = ((bf16[128,16,128]{2,1,0:T(8,128)(2,1)}), bf16[128,16,128]{2,1,0:T(8,128)(2,1)S(1)}, u32[]{:S(2)}, u32[]{:S(2)}) async-start(bf16[128,16,128]{2,1,0:T(8,128)(2,1)} %copy.319), calls=%async_computation.3 | async-start | bytes 1048576 | tf_op jit(solution)/shard_map/all_to_all | solution.py:137
  209.8 6.5 %all-to-all-done.3 = bf16[128,16,128]{2,1,0:T(8,128)(2,1)S(1)} async-done(((bf16[128,16,128]{2,1,0:T(8,128)(2,1)}), bf16[128,16,128]{2,1,0:T(8,128)(2,1)S(1)}, u32[]{:S(2)}, u32[]{:S(2)}) %all-to-all-start.3) | async-done | bytes 524320 | tf_op jit(solution)/shard_map/all_to_all | solution.py:137
  216.3 3.3 %all-to-all-start.6 = ((bf16[8,2,1024]{2,1,0:T(2,128)(2,1)}), bf16[8,2,1024]{2,1,0:T(2,128)(2,1)S(1)}, u32[]{:S(2)}, u32[]{:S(2)}) async-start(bf16[8,2,1024]{2,1,0:T(2,128)(2,1)} %reshape.976), calls=%async_computation.6 | async-start | bytes 65536 | tf_op jit(solution)/shard_map/all_to_all | solution.py:139
  220.9 4.9 %all-to-all-done.6 = bf16[8,2,1024]{2,1,0:T(2,128)(2,1)S(1)} async-done(((bf16[8,2,1024]{2,1,0:T(2,128)(2,1)}), bf16[8,2,1024]{2,1,0:T(2,128)(2,1)S(1)}, u32[]{:S(2)}, u32[]{:S(2)}) %all-to-all-start.6) | async-done | bytes 32800 | tf_op jit(solution)/shard_map/all_to_all | solution.py:139
  225.8 3.3 %all-to-all-start.7 = ((bf16[8,2,1024]{2,1,0:T(2,128)(2,1)}), bf16[8,2,1024]{2,1,0:T(2,128)(2,1)S(1)}, u32[]{:S(2)}, u32[]{:S(2)}) async-start(bf16[8,2,1024]{2,1,0:T(2,128)(2,1)} %reshape.978), calls=%async_computation.7 | async-start | bytes 65536 | tf_op jit(solution)/shard_map/all_to_all | solution.py:140
  231.5 3.8 %all-to-all-done.7 = bf16[8,2,1024]{2,1,0:T(2,128)(2,1)S(1)} async-done(((bf16[8,2,1024]{2,1,0:T(2,128)(2,1)}), bf16[8,2,1024]{2,1,0:T(2,128)(2,1)S(1)}, u32[]{:S(2)}, u32[]{:S(2)}) %all-to-all-start.7) | async-done | bytes 32800 | tf_op jit(solution)/shard_map/all_to_all | solution.py:140
  (182 shorter events, 45.4 us)
Async XLA Ops:
  2.0 5.4 %copy-start.33 = (bf16[16,8,128]{2,1,0:T(8,128)(2,1)S(1)}, bf16[16,8,128]{2,1,0:T(8,128)(2,1)}, u32[]{:S(2)}) copy-start(bf16[16,8,128]{2,1,0:T(8,128)(2,1)} %param.7) | copy-start | bytes 98308
  2.0 11.7 %all-to-all-start = ((bf16[16,8,128]{2,0,1:T(8,128)(2,1)}), bf16[16,8,128]{2,0,1:T(8,128)(2,1)S(1)}, u32[]{:S(2)}, u32[]{:S(2)}) async-start(bf16[16,8,128]{2,0,1:T(8,128)(2,1)} %copy.297), calls=%async_computation | async-start | bytes 65536 | tf_op jit(solution)/shard_map/all_to_all | solution.py:28
  13.7 9.5 %all-to-all-start.2 = ((bf16[16,8,128]{2,0,1:T(8,128)(2,1)}), bf16[16,8,128]{2,0,1:T(8,128)(2,1)S(1)}, u32[]{:S(2)}, u32[]{:S(2)}) async-start(bf16[16,8,128]{2,0,1:T(8,128)(2,1)} %copy.300), calls=%async_computation.2 | async-start | bytes 65536 | tf_op jit(solution)/shard_map/all_to_all | solution.py:29
  20.2 55.8 %copy-start.9 = (bf16[16,128,128]{2,1,0:T(8,128)(2,1)S(1)}, bf16[16,128,128]{2,1,0:T(8,128)(2,1)}, u32[]{:S(2)}) copy-start(bf16[16,128,128]{2,1,0:T(8,128)(2,1)} %param.8) | copy-start | bytes 1572868
  23.3 61.2 %all-to-all-start.1 = ((bf16[16,128,128]{2,0,1:T(8,128)(2,1)}), bf16[16,128,128]{2,0,1:T(8,128)(2,1)S(1)}, u32[]{:S(2)}, u32[]{:S(2)}) async-start(bf16[16,128,128]{2,0,1:T(8,128)(2,1)} %copy.298), calls=%async_computation.1 | async-start | bytes 1048576 | tf_op jit(solution)/shard_map/all_to_all | solution.py:27
  26.8 9.7 %collective-permute-start = (bf16[2,128,1,128]{3,1,2,0:T(8,128)(2,1)S(1)}, bf16[2,128,1,128]{3,1,2,0:T(8,128)(2,1)S(1)}, u32[]{:S(2)}, u32[]{:S(2)}) collective-permute-start(bf16[2,128,1,128]{3,1,2,0:T(8,128)(2,1)S(1)} %pad_maximum_fusion), channel_id=1, source_target_pairs={{0,8},{8,16},{16,24},{24,32},{32,40},{40,48},{48,56},{56,64},{64,7... | collective-permute-start | bytes 196616 | tf_op jit(solution)/shard_map/ppermute | solution.py:15
  36.5 9.2 %collective-permute-start.1 = (bf16[2,128,1,128]{3,1,2,0:T(8,128)(2,1)S(1)}, bf16[2,128,1,128]{3,1,2,0:T(8,128)(2,1)S(1)}, u32[]{:S(2)}, u32[]{:S(2)}) collective-permute-start(bf16[2,128,1,128]{3,1,2,0:T(8,128)(2,1)S(1)} %collective-permute-done), channel_id=1, source_target_pairs={{0,8},{8,16},{16,24},{24,32},{32,40},{40,48},{48,56},{56,64},{64,7... | collective-permute-start | bytes 196616 | tf_op jit(solution)/shard_map/ppermute | solution.py:15
  45.7 9.2 %collective-permute-start.2 = (bf16[2,128,1,128]{3,1,2,0:T(8,128)(2,1)S(1)}, bf16[2,128,1,128]{3,1,2,0:T(8,128)(2,1)S(1)}, u32[]{:S(2)}, u32[]{:S(2)}) collective-permute-start(bf16[2,128,1,128]{3,1,2,0:T(8,128)(2,1)S(1)} %collective-permute-done.1), channel_id=1, source_target_pairs={{0,8},{8,16},{16,24},{24,32},{32,40},{40,48},{48,56},{56,64},{64,7... | collective-permute-start | bytes 196616 | tf_op jit(solution)/shard_map/ppermute | solution.py:15
  54.9 9.2 %collective-permute-start.3 = (bf16[2,128,1,128]{3,1,2,0:T(8,128)(2,1)S(1)}, bf16[2,128,1,128]{3,1,2,0:T(8,128)(2,1)S(1)}, u32[]{:S(2)}, u32[]{:S(2)}) collective-permute-start(bf16[2,128,1,128]{3,1,2,0:T(8,128)(2,1)S(1)} %collective-permute-done.2), channel_id=1, source_target_pairs={{0,8},{8,16},{16,24},{24,32},{32,40},{40,48},{48,56},{56,64},{64,7... | collective-permute-start | bytes 196616 | tf_op jit(solution)/shard_map/ppermute | solution.py:15
  64.0 9.2 %collective-permute-start.4 = (bf16[2,128,1,128]{3,1,2,0:T(8,128)(2,1)S(1)}, bf16[2,128,1,128]{3,1,2,0:T(8,128)(2,1)S(1)}, u32[]{:S(2)}, u32[]{:S(2)}) collective-permute-start(bf16[2,128,1,128]{3,1,2,0:T(8,128)(2,1)S(1)} %collective-permute-done.3), channel_id=1, source_target_pairs={{0,8},{8,16},{16,24},{24,32},{32,40},{40,48},{48,56},{56,64},{64,7... | collective-permute-start | bytes 196616 | tf_op jit(solution)/shard_map/ppermute | solution.py:15
  73.2 9.3 %collective-permute-start.5 = (bf16[2,128,1,128]{3,1,2,0:T(8,128)(2,1)S(1)}, bf16[2,128,1,128]{3,1,2,0:T(8,128)(2,1)}, u32[]{:S(2)}, u32[]{:S(2)}) collective-permute-start(bf16[2,128,1,128]{3,1,2,0:T(8,128)(2,1)S(1)} %collective-permute-done.4), channel_id=1, source_target_pairs={{0,8},{8,16},{16,24},{24,32},{32,40},{40,48},{48,56},{56,64},{64,7... | collective-permute-start | bytes 196616 | tf_op jit(solution)/shard_map/ppermute | solution.py:15
  76.0 13.7 %copy-start.22 = (pred[128,128]{0,1:T(8,128)(4,1)}, pred[128,128]{0,1:T(8,128)(4,1)S(1)}, u32[]{:S(2)}) copy-start(pred[128,128]{0,1:T(8,128)(4,1)S(1)} %get-tuple-element.39) | copy-start | bytes 49156
  82.5 25.3 %collective-permute-start.6 = (bf16[2,128,1,128]{3,1,2,0:T(8,128)(2,1)}, bf16[2,128,1,128]{3,1,2,0:T(8,128)(2,1)}, u32[]{:S(2)}, u32[]{:S(2)}) collective-permute-start(bf16[2,128,1,128]{3,1,2,0:T(8,128)(2,1)} %collective-permute-done.5), channel_id=1, source_target_pairs={{0,8},{8,16},{16,24},{24,32},{32,40},{40,48},{48,56},{56,64},{64,7... | collective-permute-start | bytes 196616 | tf_op jit(solution)/shard_map/ppermute | solution.py:15
  84.5 17.8 %all-to-all-start.4 = ((bf16[16,128,128]{2,0,1:T(8,128)(2,1)}), bf16[16,128,128]{2,0,1:T(8,128)(2,1)S(1)}, u32[]{:S(2)}, u32[]{:S(2)}) async-start(bf16[16,128,128]{2,0,1:T(8,128)(2,1)} %copy.321), calls=%async_computation.4 | async-start | bytes 1048576 | tf_op jit(solution)/shard_map/all_to_all | solution.py:30
  90.0 11.5 %copy-start.24 = (f32[16,128]{1,0:T(8,128)}, f32[16,128]{1,0:T(8,128)S(1)}, u32[]{:S(2)}) copy-start(f32[16,128]{1,0:T(8,128)S(1)} %get-tuple-element.54) | copy-start | bytes 24580
  90.4 1.7 copy-start.16
  92.1 1.9 copy-start.14
  93.9 1.9 copy-start.12
  95.8 1.9 copy-start.10
  102.3 0.8 copy-start.7
  106.7 3.2 %copy-start.20 = (pred[128,128]{0,1:T(8,128)(4,1)S(1)}, pred[128,128]{0,1:T(8,128)(4,1)}, u32[]{:S(2)}) copy-start(pred[128,128]{0,1:T(8,128)(4,1)} %get-tuple-element.37) | copy-start | bytes 49156
  107.8 9.7 %collective-permute-start.7 = (bf16[2,128,1,128]{3,1,2,0:T(8,128)(2,1)}, bf16[2,128,1,128]{3,1,2,0:T(8,128)(2,1)S(1)}, u32[]{:S(2)}, u32[]{:S(2)}) collective-permute-start(bf16[2,128,1,128]{3,1,2,0:T(8,128)(2,1)} %collective-permute-done.6), channel_id=1, source_target_pairs={{0,8},{8,16},{16,24},{24,32},{32,40},{40,48},{48,56},{56,64},{64,7... | collective-permute-start | bytes 196616 | tf_op jit(solution)/shard_map/ppermute | solution.py:15
  110.0 7.7 %copy-start.21 = (pred[128,128]{0,1:T(8,128)(4,1)S(1)}, pred[128,128]{0,1:T(8,128)(4,1)}, u32[]{:S(2)}) copy-start(pred[128,128]{0,1:T(8,128)(4,1)} %get-tuple-element.38) | copy-start | bytes 49156
  111.1 7.3 %copy-start.4 = (f32[1,16,128,128]{2,3,1,0:T(8,128)S(1)}, f32[1,16,128,128]{2,3,1,0:T(8,128)}, u32[]{:S(2)}) copy-start(f32[1,16,128,128]{2,3,1,0:T(8,128)} %get-tuple-element.57) | copy-start | bytes 3145732
  117.6 0.8 copy-start.31
  117.6 0.8 copy-start.32
  117.6 1.3 copy-start.3
  118.4 1.3 copy-start.2
  118.9 1.3 copy-start.1
  119.7 1.3 copy-start
  122.2 0.8 copy-start.17
  122.2 0.8 copy-start.19
  122.2 0.8 copy-start.23
  124.7 6.1 %copy-start.5 = (bf16[1,16,128,128]{2,3,1,0:T(8,128)(2,1)}, bf16[1,16,128,128]{2,3,1,0:T(8,128)(2,1)S(1)}, u32[]{:S(2)}) copy-start(bf16[1,16,128,128]{2,3,1,0:T(8,128)(2,1)S(1)} %get-tuple-element.30) | copy-start | bytes 1572868
  129.2 1.2 copy-start.8
  131.8 12.3 %collective-permute-start.8 = (bf16[2,128,1,128]{3,1,2,0:T(8,128)(2,1)S(1)}, bf16[2,128,1,128]{3,1,2,0:T(8,128)(2,1)S(1)}, u32[]{:S(2)}, u32[]{:S(2)}) collective-permute-start(bf16[2,128,1,128]{3,1,2,0:T(8,128)(2,1)S(1)} %pad_maximum_fusion.1), channel_id=1, source_target_pairs={{8,0},{16,8},{24,16},{32,24},{40,32},{48,40},{56,48},{64,56},{72,6... | collective-permute-start | bytes 196616 | tf_op jit(solution)/shard_map/ppermute | solution.py:15
  144.1 3.9 %collective-permute-start.9 = (bf16[2,128,1,128]{3,1,2,0:T(8,128)(2,1)S(1)}, bf16[2,128,1,128]{3,1,2,0:T(8,128)(2,1)S(1)}, u32[]{:S(2)}, u32[]{:S(2)}) collective-permute-start(bf16[2,128,1,128]{3,1,2,0:T(8,128)(2,1)S(1)} %fusion.88), channel_id=1, source_target_pairs={{8,0},{16,8},{24,16},{32,24},{40,32},{48,40},{56,48},{64,56},{72,6... | collective-permute-start | bytes 196616 | tf_op jit(solution)/shard_map/ppermute | solution.py:15
  148.1 9.2 %collective-permute-start.10 = (bf16[2,128,1,128]{3,1,2,0:T(8,128)(2,1)S(1)}, bf16[2,128,1,128]{3,1,2,0:T(8,128)(2,1)S(1)}, u32[]{:S(2)}, u32[]{:S(2)}) collective-permute-start(bf16[2,128,1,128]{3,1,2,0:T(8,128)(2,1)S(1)} %fusion.89), channel_id=1, source_target_pairs={{8,0},{16,8},{24,16},{32,24},{40,32},{48,40},{56,48},{64,56},{72,6... | collective-permute-start | bytes 196616 | tf_op jit(solution)/shard_map/ppermute | solution.py:15
  157.3 9.2 %collective-permute-start.11 = (bf16[2,128,1,128]{3,1,2,0:T(8,128)(2,1)S(1)}, bf16[2,128,1,128]{3,1,2,0:T(8,128)(2,1)S(1)}, u32[]{:S(2)}, u32[]{:S(2)}) collective-permute-start(bf16[2,128,1,128]{3,1,2,0:T(8,128)(2,1)S(1)} %fusion.90), channel_id=1, source_target_pairs={{8,0},{16,8},{24,16},{32,24},{40,32},{48,40},{56,48},{64,56},{72,6... | collective-permute-start | bytes 196616 | tf_op jit(solution)/shard_map/ppermute | solution.py:15
  166.5 9.2 %collective-permute-start.12 = (bf16[2,128,1,128]{3,1,2,0:T(8,128)(2,1)S(1)}, bf16[2,128,1,128]{3,1,2,0:T(8,128)(2,1)S(1)}, u32[]{:S(2)}, u32[]{:S(2)}) collective-permute-start(bf16[2,128,1,128]{3,1,2,0:T(8,128)(2,1)S(1)} %fusion.91), channel_id=1, source_target_pairs={{8,0},{16,8},{24,16},{32,24},{40,32},{48,40},{56,48},{64,56},{72,6... | collective-permute-start | bytes 196616 | tf_op jit(solution)/shard_map/ppermute | solution.py:15
  175.7 14.0 %collective-permute-start.13 = (bf16[2,128,1,128]{3,1,2,0:T(8,128)(2,1)S(1)}, bf16[2,128,1,128]{3,1,2,0:T(8,128)(2,1)S(1)}, u32[]{:S(2)}, u32[]{:S(2)}) collective-permute-start(bf16[2,128,1,128]{3,1,2,0:T(8,128)(2,1)S(1)} %fusion.92), channel_id=1, source_target_pairs={{8,0},{16,8},{24,16},{32,24},{40,32},{48,40},{56,48},{64,56},{72,6... | collective-permute-start | bytes 196616 | tf_op jit(solution)/shard_map/ppermute | solution.py:15
  184.5 17.6 %all-to-all-start.5 = ((bf16[128,16,128]{2,1,0:T(8,128)(2,1)}), bf16[128,16,128]{2,1,0:T(8,128)(2,1)S(1)}, u32[]{:S(2)}, u32[]{:S(2)}) async-start(bf16[128,16,128]{2,1,0:T(8,128)(2,1)} %copy.351), calls=%async_computation.5 | async-start | bytes 1048576 | tf_op jit(solution)/shard_map/all_to_all | solution.py:138
  189.8 4.4 %collective-permute-start.14 = (bf16[2,128,1,128]{3,1,2,0:T(8,128)(2,1)S(1)}, bf16[2,128,1,128]{3,1,2,0:T(8,128)(2,1)S(1)}, u32[]{:S(2)}, u32[]{:S(2)}) collective-permute-start(bf16[2,128,1,128]{3,1,2,0:T(8,128)(2,1)S(1)} %fusion.93), channel_id=1, source_target_pairs={{8,0},{16,8},{24,16},{32,24},{40,32},{48,40},{56,48},{64,56},{72,6... | collective-permute-start | bytes 196616 | tf_op jit(solution)/shard_map/ppermute | solution.py:15
  194.2 13.4 %copy-start.6 = (bf16[1,16,128,128]{2,3,1,0:T(8,128)(2,1)S(1)}, bf16[1,16,128,128]{2,3,1,0:T(8,128)(2,1)}, u32[]{:S(2)}) copy-start(bf16[1,16,128,128]{2,3,1,0:T(8,128)(2,1)} %copy-done.5) | copy-start | bytes 1572868
  194.2 13.7 %collective-permute-start.15 = (bf16[2,128,1,128]{3,1,2,0:T(8,128)(2,1)S(1)}, bf16[2,128,1,128]{3,1,2,0:T(8,128)(2,1)S(1)}, u32[]{:S(2)}, u32[]{:S(2)}) collective-permute-start(bf16[2,128,1,128]{3,1,2,0:T(8,128)(2,1)S(1)} %fusion.94), channel_id=1, source_target_pairs={{8,0},{16,8},{24,16},{32,24},{40,32},{48,40},{56,48},{64,56},{72,6... | collective-permute-start | bytes 196616 | tf_op jit(solution)/shard_map/ppermute | solution.py:15
  202.1 14.2 %all-to-all-start.3 = ((bf16[128,16,128]{2,1,0:T(8,128)(2,1)}), bf16[128,16,128]{2,1,0:T(8,128)(2,1)S(1)}, u32[]{:S(2)}, u32[]{:S(2)}) async-start(bf16[128,16,128]{2,1,0:T(8,128)(2,1)} %copy.319), calls=%async_computation.3 | async-start | bytes 1048576 | tf_op jit(solution)/shard_map/all_to_all | solution.py:137
  216.3 9.5 %all-to-all-start.6 = ((bf16[8,2,1024]{2,1,0:T(2,128)(2,1)}), bf16[8,2,1024]{2,1,0:T(2,128)(2,1)S(1)}, u32[]{:S(2)}, u32[]{:S(2)}) async-start(bf16[8,2,1024]{2,1,0:T(2,128)(2,1)} %reshape.976), calls=%async_computation.6 | async-start | bytes 65536 | tf_op jit(solution)/shard_map/all_to_all | solution.py:139
  225.8 9.5 %all-to-all-start.7 = ((bf16[8,2,1024]{2,1,0:T(2,128)(2,1)}), bf16[8,2,1024]{2,1,0:T(2,128)(2,1)S(1)}, u32[]{:S(2)}, u32[]{:S(2)}) async-start(bf16[8,2,1024]{2,1,0:T(2,128)(2,1)} %reshape.978), calls=%async_computation.7 | async-start | bytes 65536 | tf_op jit(solution)/shard_map/all_to_all | solution.py:140
  (11 other events, 7.9 us)
where the time goes:
time: 238 us; the launch traced here: 236 us
  starting transfers between devices  94.2 us (40%)
  waiting for transfers between devices  79.4 us (33%)
  matrix products  31.7 us (13%)
  local copies, waits for them, and re-layouts  22.8 us (10%)
  other arithmetic  6.35 us (3%)
    ppermute x16, starting transfers between devices, shifted(): return lax.ppermute(block, axis, route)  59.3 us
    ppermute x16, waiting for transfers between devices, shifted(): return lax.ppermute(block, axis, route)  55.4 us
    unnamed x82, local copies, waits for them, and re-layouts  13.3 us
    dot_general x9, matrix products, block_scores(): jnp.einsum('tkgd,skd->kgts', grouped, pair[0], preferred_element_type=jnp...  12.8 us
    all_to_all x1, waiting for transfers between devices, on_device(): lax.all_to_all(attended_flat, 'head', split_axis=0, concat_axis=1, tiled=...  6.54 us
    all_to_all x1, waiting for transfers between devices, on_device(): lax.all_to_all(key, 'head', split_axis=1, concat_axis=0, tiled=True)  5.63 us
    all_to_all x1, starting transfers between devices, on_device(): lax.all_to_all(attended_flat, 'head', split_axis=0, concat_axis=1, tiled=...  5.5 us
    all_to_all x1, starting transfers between devices, on_device(): lax.all_to_all(key, 'head', split_axis=1, concat_axis=0, tiled=True)  5.44 us
  transfers between devices with their start and end apart: 24, of which 17 were waited for; matrix products, arithmetic and copies ran while one was open for 18% of the time, Pallas kernels for 0%

commit v1 on v0

v1 whole, which is shorter than its diff:
```python
import jax
import jax.numpy as jnp
from jax import lax
from jax.experimental import pallas as pl
from jax.experimental.pallas import tpu as pltpu
from jax.sharding import Mesh, PartitionSpec as P

REACH = 8
NEGATIVE = -1e30
LOG2E = 1.4426950408889634
CORES = 2
QUARTERS = 4
SPANS = REACH // QUARTERS + 1


def dot(a, b, dims):
    return lax.dot_general(a, b, (dims, ((), ())), preferred_element_type=jnp.float32)


def attention_kernel(
    places, lengths, moved, same_core, other_core, out_moved, out_window,
    keys, values, keys_t, values_t, key_sum, value_sum, weight_all, dscore_all,
):
    chunks, _, group, width = moved.shape
    chunk_tok = moved.shape[1] // 2
    rows = chunk_tok * group
    block = chunks * chunk_tok
    span = (REACH + 1) * block
    inv_root = width ** (-0.5)
    scale = inv_root * LOG2E
    z_place, quarter = places[0], places[1]
    window_first = (z_place * QUARTERS + quarter - REACH) * block

    for index in range(REACH + 1):
        place = quarter + index
        near, old = lax.rem(place, QUARTERS), SPANS - 1 - lax.div(place, QUARTERS)
        side = lax.div(near, CORES)
        at_home = lax.rem(near, CORES) == lax.rem(quarter, CORES)
        part = pl.ds(index * block, block)
        key_block = jnp.where(
            at_home, same_core[old, side, :, 0], other_core[old, side, :, 0]
        ).reshape(block, width)
        value_block = jnp.where(
            at_home, same_core[old, side, :, 1], other_core[old, side, :, 1]
        ).reshape(block, width)
        keys[part, :] = key_block
        values[part, :] = value_block
        keys_t[:, part] = key_block.T
        values_t[:, part] = value_block.T

    token = lax.broadcasted_iota(jnp.int32, (1, rows), 1) // group

    def first_keys(chunk):
        position = token + (REACH * block + chunk * chunk_tok) + window_first
        begin = jnp.int32(0)
        start = jnp.zeros((1, rows), jnp.int32)
        for doc in range(lengths.shape[0]):
            start = jnp.where(position >= begin, begin, start)
            begin = begin + lengths[doc]
        return start - window_first

    def part_of(index):
        return pl.ds(index * block, block)

    def lanes_of(chunk):
        return pl.ds(chunk * rows, rows)

    def operands(chunk):
        query = moved[chunk, :chunk_tok].reshape(rows, width)
        grad = moved[chunk, chunk_tok:].reshape(rows, width)
        return query, grad

    def live(index, chunk):
        low = chunk * chunk_tok if index == 0 else 0
        high = (chunk + 1) * chunk_tok if index == REACH else block
        return low, high

    def rows_of(index, chunk):
        low, high = live(index, chunk)
        return pl.ds(index * block + low, high - low)

    def clear(held, chunk):
        before, after = chunk * chunk_tok, block - (chunk + 1) * chunk_tok
        if before:
            held[pl.ds(0, before), lanes_of(chunk)] = jnp.zeros((before, rows), held.dtype)
        if after:
            held[pl.ds(span - after, after), lanes_of(chunk)] = jnp.zeros((after, rows), held.dtype)

    state = {}

    def forward(chunk):
        query, _ = operands(chunk)
        low = first_keys(chunk)
        highest, total, seen = None, None, {}
        for index in [REACH] + list(range(REACH)):
            scores = dot(keys[rows_of(index, chunk), :], query, ((1,), (1,)))
            first, last = live(index, chunk)
            key_row = lax.broadcasted_iota(jnp.int32, (last - first, rows), 0) + first
            allowed = key_row >= low - index * block
            if index == REACH:
                allowed = allowed & (key_row <= token + chunk * chunk_tok)
            scores = jnp.where(allowed, scores, NEGATIVE)
            most = jnp.max(scores, axis=0, keepdims=True)
            if highest is None:
                weights = jnp.exp2((scores - most) * scale)
                total = jnp.sum(weights, axis=0, keepdims=True)
            else:
                most = jnp.maximum(most, highest)
                weights = jnp.exp2((scores - most) * scale)
                total = total * jnp.exp2((highest - most) * scale)
                total = total + jnp.sum(weights, axis=0, keepdims=True)
            highest = most
            seen[index] = most
            weight_all[rows_of(index, chunk), lanes_of(chunk)] = weights.astype(jnp.bfloat16)
            yield
        clear(weight_all, chunk)
        inverse = 1.0 / total
        state[chunk] = {
            index: jnp.exp2((most - highest) * scale) * inverse for index, most in seen.items()
        }

    def backward(chunk):
        query, grad = operands(chunk)
        factors = state.pop(chunk)
        for index in range(REACH + 1):
            part = rows_of(index, chunk)
            weights = weight_all[part, lanes_of(chunk)].astype(jnp.float32)
            weight_all[part, lanes_of(chunk)] = (weights * factors[index]).astype(jnp.bfloat16)
            if index % 3 == 2:
                yield
        attended = dot(values_t[...], weight_all[:, lanes_of(chunk)], ((1,), (0,)))
        attended = attended.astype(jnp.bfloat16)
        out_moved[chunk, :chunk_tok] = attended.T.reshape(chunk_tok, group, width)
        delta = jnp.sum(
            grad.T.astype(jnp.float32) * attended.astype(jnp.float32), axis=0, keepdims=True
        )
        yield
        for index in range(REACH + 1):
            part = rows_of(index, chunk)
            dprob = dot(values[part, :], grad, ((1,), (1,)))
            weights = weight_all[part, lanes_of(chunk)].astype(jnp.float32)
            dscore_all[part, lanes_of(chunk)] = (weights * (dprob - delta)).astype(jnp.bfloat16)
            yield
        clear(dscore_all, chunk)
        query_grad = dot(keys_t[...], dscore_all[:, lanes_of(chunk)], ((1,), (0,))) * inv_root
        query_grad = query_grad.astype(jnp.bfloat16)
        out_moved[chunk, chunk_tok : 2 * chunk_tok] = query_grad.T.reshape(chunk_tok, group, width)
        yield

    def gather(first, count):
        lanes = pl.ds(first * rows, count * rows)
        chosen = pl.ds(first, count)
        query = moved[chosen, :chunk_tok].reshape(count * rows, width)
        grad = moved[chosen, chunk_tok:].reshape(count * rows, width)
        for index in range(REACH + 1):
            part = part_of(index)
            value_part = dot(weight_all[part, lanes], grad, ((1,), (0,)))
            key_part = dot(dscore_all[part, lanes], query, ((1,), (0,)))
            if first:
                value_part = value_part + value_sum[part, :]
                key_part = key_part + key_sum[part, :]
            value_sum[part, :] = value_part
            key_sum[part, :] = key_part
            if index % 3 == 2:
                yield

    def together(*streams):
        streams = list(streams)
        while streams:
            for stream in list(streams):
                if next(stream, streams) is streams:
                    streams.remove(stream)

    together(forward(0))
    for chunk in range(chunks):
        streams = [backward(chunk)]
        if chunk + 1 < chunks:
            streams.append(forward(chunk + 1))
        if chunk and chunk % 2 == 0:
            streams.append(gather(chunk - 2, 2))
        if chunk == chunks - 1:
            streams.append(gather(chunk - 1, 1))
        together(*streams)
    together(gather(chunks - 1, 1))

    shape = (chunks, chunk_tok, width)
    blank = jnp.zeros((chunks, 2, chunk_tok, width), out_window.dtype)
    for index in range(QUARTERS * SPANS):
        place = lax.rem(quarter + index, QUARTERS * SPANS)
        near, plane = lax.rem(place, QUARTERS), lax.div(place, QUARTERS)
        away = lax.rem(near + quarter, CORES)
        side = lax.div(near, CORES)
        if index <= REACH:
            part = part_of(index)
            out_window[away, plane, side, :, 0] = (key_sum[part, :] * inv_root).reshape(shape)
            out_window[away, plane, side, :, 1] = value_sum[part, :].reshape(shape)
        else:
            out_window[away, plane, side] = blank


def attention(places, lengths, moved, same_core, other_core):
    chunks, twice, group, width = moved.shape
    chunk_tok = twice // 2
    block = chunks * chunk_tok
    span = (REACH + 1) * block
    vmem = pl.BlockSpec(memory_space=pltpu.VMEM)
    smem = pl.BlockSpec(memory_space=pltpu.SMEM)
    return pl.pallas_call(
        attention_kernel,
        out_shape=(
            jax.ShapeDtypeStruct(moved.shape, jnp.bfloat16),
            jax.ShapeDtypeStruct((CORES,) + same_core.shape, jnp.float32),
        ),
        in_specs=[smem, smem, vmem, vmem, vmem],
        out_specs=(vmem, vmem),
        scratch_shapes=[
            pltpu.VMEM((span, width), jnp.bfloat16),
            pltpu.VMEM((span, width), jnp.bfloat16),
            pltpu.VMEM((width, span), jnp.bfloat16),
            pltpu.VMEM((width, span), jnp.bfloat16),
            pltpu.VMEM((span, width), jnp.float32),
            pltpu.VMEM((span, width), jnp.float32),
            pltpu.VMEM((span, block * group), jnp.bfloat16),
            pltpu.VMEM((span, block * group), jnp.bfloat16),
        ],
        compiler_params=pltpu.CompilerParams(vmem_limit_bytes=40 * 1024 * 1024),
        cost_estimate=pl.CostEstimate(
            flops=12 * block * group * span * width,
            bytes_accessed=4 * moved.size + 4 * same_core.size,
            transcendentals=block * group * span,
        ),
        name="attention",
    )(places, lengths, moved, same_core, other_core)


def spread_kernel(back, attended, query_grad, sems):
    kv_heads, _, group, _ = back.shape
    tokens = attended.shape[0]
    copies = []
    for index in range(kv_heads):
        heads = pl.ds(index * group, group)
        for which, target in enumerate((attended, query_grad)):
            copies.append(
                pltpu.make_async_copy(
                    back.at[index, pl.ds(which * tokens, tokens)],
                    target.at[:, heads, :],
                    sems.at[2 * index + which],
                )
            )
            copies[-1].start()
    for copy in copies:
        copy.wait()


def spread(back, query):
    anywhere = pl.BlockSpec(memory_space=pl.ANY)
    large = jax.ShapeDtypeStruct(query.shape, jnp.bfloat16)
    return pl.pallas_call(
        spread_kernel,
        out_shape=(large, large),
        in_specs=[pl.BlockSpec(memory_space=pltpu.VMEM)],
        out_specs=(anywhere, anywhere),
        scratch_shapes=[pltpu.SemaphoreType.DMA((2 * back.shape[0],))],
        compiler_params=pltpu.CompilerParams(vmem_limit_bytes=16 * 1024 * 1024),
        name="spread",
    )(back)


def split_kernel(total, key_grad, value_grad, spread):
    for which, target in enumerate((key_grad, value_grad)):
        for index in range(total.shape[1]):
            both = total[0, index, which].astype(jnp.float32)
            spread[:, index, :] = both + total[1, index, which].astype(jnp.float32)
        target[...] = spread[...].astype(jnp.bfloat16)


def split(total, key):
    vmem = pl.BlockSpec(memory_space=pltpu.VMEM)
    small = jax.ShapeDtypeStruct(key.shape, jnp.bfloat16)
    return pl.pallas_call(
        split_kernel,
        out_shape=(small, small),
        in_specs=[vmem],
        out_specs=(vmem, vmem),
        scratch_shapes=[pltpu.VMEM(key.shape, jnp.float32)],
        compiler_params=pltpu.CompilerParams(vmem_limit_bytes=16 * 1024 * 1024),
        name="split",
    )(total)


def turned(block, axis, distance):
    size = lax.axis_size(axis)
    return lax.ppermute(block, axis, [(i, (i + distance) % size) for i in range(size)])


def swapped(block):
    return lax.all_to_all(block, "head", split_axis=0, concat_axis=0, tiled=True)


def crossed(block):
    flat = block.reshape((-1,) + block.shape[2:])
    flat = lax.all_to_all(flat, ("yhi", "head"), split_axis=0, concat_axis=0, tiled=True)
    return flat.reshape(block.shape)


def on_device(query, key, value, out_grad, doc_lengths):
    tokens, heads, width = query.shape
    kv_heads = key.shape[1]
    group = heads // kv_heads

    pair = jnp.transpose(jnp.stack([key, value]), (2, 0, 1, 3))
    pair = crossed(jnp.broadcast_to(pair[None], (QUARTERS // CORES,) + pair.shape))
    both = jnp.stack([query, out_grad]).reshape(2 * tokens, kv_heads, group, width)
    both = jnp.transpose(both, (1, 0, 2, 3))
    pair, both = lax.optimization_barrier((pair, both))
    moved = swapped(both)
    layers = [pair] + [turned(pair, "z", distance) for distance in range(1, SPANS)]
    same_core = jnp.stack(layers)
    other_core = turned(same_core, "core", 1)

    quarter = lax.axis_index("yhi") * CORES + lax.axis_index("core")
    places = jnp.stack([lax.axis_index("z"), quarter]).astype(jnp.int32)
    out_moved, out_window = attention(places, doc_lengths, moved, same_core, other_core)

    back = swapped(out_moved)
    beside = turned(out_window[1].astype(jnp.bfloat16), "core", 1)
    own = out_window[0] + beside.astype(jnp.float32)
    total = own[SPANS - 1]
    for distance in range(1, SPANS):
        sent = turned(own[SPANS - 1 - distance].astype(jnp.bfloat16), "z", -distance)
        total = total + sent.astype(jnp.float32)
    back, total = lax.optimization_barrier((back, total.astype(jnp.bfloat16)))
    total = crossed(total)
    attended, query_grad = spread(back, query)
    key_grad, value_grad = split(total, key)
    return attended, query_grad, key_grad, value_grad


def solution(mesh):
    ctx, head = mesh.devices.shape
    finer = Mesh(
        mesh.devices.reshape(ctx // QUARTERS, QUARTERS // CORES, CORES, head),
        ("z", "yhi", "core", "head"),
    )
    token_split = P(("z", "yhi", "core", "head"), None, None)
    return jax.shard_map(
        on_device,
        mesh=finer,
        in_specs=(token_split,) * 4 + (P(),),
        out_specs=(token_split,) * 4,
        check_vma=False,
    )
```

time: 238 us -> 90.2 us (0.38)
  the two profiles are of different devices: /device:TPU:256 before, /device:TPU:1 now
where the time goes in v1:
time: 90.2 us; the launch traced here: 89.3 us
  starting transfers between devices  41.3 us (46%)
  waiting for transfers between devices  30.1 us (33%)
  Pallas kernels  12.2 us (14%)
  other arithmetic  3.08 us (3%)
  local copies, waits for them, and re-layouts  1.94 us (2%)
    ppermute x6, starting transfers between devices, turned(): lax.ppermute(block, axis, [(i, (i + distance) % size) for i in range(size)])  21.6 us
    ppermute x6, waiting for transfers between devices, turned(): lax.ppermute(block, axis, [(i, (i + distance) % size) for i in range(size)])  18.4 us
    all_to_all x2, starting transfers between devices, crossed(): lax.all_to_all(flat, ('yhi', 'head'), split_axis=0, concat_axis=0, tiled=...  11.1 us
    pallas_call x1, Pallas kernels, attention(): pl.pallas_call(attention_kernel, out_shape=(jax.ShapeDtypeStruct(moved.sh...  10.4 us
    all_to_all x2, waiting for transfers between devices, crossed(): lax.all_to_all(flat, ('yhi', 'head'), split_axis=0, concat_axis=0, tiled=...  10.1 us
    all_to_all x2, starting transfers between devices, swapped(): lax.all_to_all(block, 'head', split_axis=0, concat_axis=0, tiled=True)  8.63 us
  transfers between devices with their start and end apart: 10, of which 7 were waited for; matrix products, arithmetic and copies ran while one was open for 4% of the time, Pallas kernels for 1%

profile of v1, /device:TPU:1, one launch (start us, length us, event | category | flops | bytes accessed | tf_op | source)
XLA Modules:
  0.0 89.3 jit_solution(3650816519492318425)
XLA Ops:
  0.6 0.8 maximum_bitcast_fusion
  1.4 0.7 broadcast_in_dim.2
  2.1 7.6 %all-to-all-start = ((bf16[16,2,16,128]{3,2,1,0:T(8,128)(2,1)}), bf16[16,2,16,128]{3,2,1,0:T(8,128)(2,1)S(1)}, u32[]{:S(2)}, u32[]{:S(2)}) async-start(bf16[16,2,16,128]{3,2,1,0:T(8,128)(2,1)} %bitcast.5), calls=%async_computation | async-start | bytes 262144 | tf_op jit(solution)/shard_map/all_to_all | solution.py:302
  9.7 1.3 %pad_maximum_fusion = bf16[2,16,128,128]{3,2,1,0:T(8,128)(2,1)S(1)} fusion(bf16[1,16,128,128]{3,2,1,0:T(8,128)(2,1)} %bitcast.41, bf16[1,16,128,128]{3,2,1,0:T(8,128)(2,1)} %bitcast.42), kind=kLoop, calls=%fused_computation | loop fusion | flops 524288 | bytes 2097152 | tf_op jit(solution)/shard_map/stack | solution.py:313
  11.0 1.2 %copy.13 = bf16[32,8,16,128]{3,2,0,1:T(8,128)(2,1)} copy(bf16[32,8,16,128]{3,2,1,0:T(8,128)(2,1)S(1)} %bitcast.37) | data formatting | bytes 2097152 | tf_op jit(solution)/shard_map/reshape | solution.py:313
  12.2 0.0 copy-start
  12.2 4.4 %all-to-all-done = bf16[16,2,16,128]{3,2,1,0:T(8,128)(2,1)S(1)} async-done(((bf16[16,2,16,128]{3,2,1,0:T(8,128)(2,1)}), bf16[16,2,16,128]{3,2,1,0:T(8,128)(2,1)S(1)}, u32[]{:S(2)}, u32[]{:S(2)}) %all-to-all-start) | async-done | bytes 131104 | tf_op jit(solution)/shard_map/all_to_all | solution.py:302
  16.5 3.6 %all-to-all-start.1 = ((bf16[8,32,16,128]{3,2,1,0:T(8,128)(2,1)}), bf16[8,32,16,128]{3,2,1,0:T(8,128)(2,1)S(1)}, u32[]{:S(2)}, u32[]{:S(2)}) async-start(bf16[8,32,16,128]{3,2,1,0:T(8,128)(2,1)} %bitcast.35), calls=%async_computation.1 | async-start | bytes 2097152 | tf_op jit(solution)/shard_map/all_to_all | solution.py:297
  20.1 4.9 %collective-permute-start.1 = (bf16[2,8,2,16,128]{4,3,2,1,0:T(8,128)(2,1)S(1)}, bf16[2,8,2,16,128]{4,3,2,1,0:T(8,128)(2,1)S(1)}, u32[]{:S(2)}, u32[]{:S(2)}) collective-permute-start(bf16[2,8,2,16,128]{4,3,2,1,0:T(8,128)(2,1)S(1)} %bitcast.38), channel_id=1, source_target_pairs={{0,64},{32,96},{64,128},{96,160},{128,192},{160,224},{192,256},{22... | collective-permute-start | bytes 393224 | tf_op jit(solution)/shard_map/ppermute | solution.py:293
  25.0 3.5 %collective-permute-start = (bf16[2,8,2,16,128]{4,3,2,1,0:T(8,128)(2,1)S(1)}, bf16[2,8,2,16,128]{4,3,2,1,0:T(8,128)(2,1)S(1)}, u32[]{:S(2)}, u32[]{:S(2)}) collective-permute-start(bf16[2,8,2,16,128]{4,3,2,1,0:T(8,128)(2,1)S(1)} %bitcast.39), channel_id=1, source_target_pairs={{0,32},{32,64},{64,96},{96,128},{128,160},{160,192},{192,224},{224... | collective-permute-start | bytes 393224 | tf_op jit(solution)/shard_map/ppermute | solution.py:293
  28.6 5.6 %collective-permute-done.1 = bf16[2,8,2,16,128]{4,3,2,1,0:T(8,128)(2,1)S(1)} collective-permute-done((bf16[2,8,2,16,128]{4,3,2,1,0:T(8,128)(2,1)S(1)}, bf16[2,8,2,16,128]{4,3,2,1,0:T(8,128)(2,1)S(1)}, u32[]{:S(2)}, u32[]{:S(2)}) %collective-permute-start.1) | collective-permute-done | bytes 131104 | tf_op jit(solution)/shard_map/ppermute | solution.py:293
  34.1 5.9 %collective-permute-done = bf16[2,8,2,16,128]{4,3,2,1,0:T(8,128)(2,1)S(1)} collective-permute-done((bf16[2,8,2,16,128]{4,3,2,1,0:T(8,128)(2,1)S(1)}, bf16[2,8,2,16,128]{4,3,2,1,0:T(8,128)(2,1)S(1)}, u32[]{:S(2)}, u32[]{:S(2)}) %collective-permute-start) | collective-permute-done | bytes 131104 | tf_op jit(solution)/shard_map/ppermute | solution.py:293
  40.0 3.2 %collective-permute-start.2 = (bf16[3,2,8,2,16,128]{5,4,3,2,1,0:T(8,128)(2,1)S(1)}, bf16[3,2,8,2,16,128]{5,4,3,2,1,0:T(8,128)(2,1)S(1)}, u32[]{:S(2)}, u32[]{:S(2)}) collective-permute-start(bf16[3,2,8,2,16,128]{5,4,3,2,1,0:T(8,128)(2,1)S(1)} %pad_maximum_fusion.1.same_core), channel_id=1, source_target_pairs={{0,8},{8,0},{1,9},{9,1},{2,10},{10,2},{3,11},{11,3},{4,12},{12,4},... | collective-permute-start | bytes 1179656 | tf_op jit(solution)/shard_map/ppermute | solution.py:293
  43.3 0.1 pad_add_fusion.places
  43.4 1.2 %collective-permute-done.2.other_core = bf16[3,2,8,2,16,128]{5,4,3,2,1,0:T(8,128)(2,1)S(1)} collective-permute-done((bf16[3,2,8,2,16,128]{5,4,3,2,1,0:T(8,128)(2,1)S(1)}, bf16[3,2,8,2,16,128]{5,4,3,2,1,0:T(8,128)(2,1)S(1)}, u32[]{:S(2)}, u32[]{:S(2)}) %collective-permute-start.2) | collective-permute-done | bytes 393248 | tf_op jit(solution)/shard_map/ppermute | solution.py:293
  44.6 0.0 all-to-all-done.1.moved
  44.6 0.0 copy-done
  44.6 10.4 %attention.1 = (bf16[8,32,16,128]{3,2,1,0:T(8,128)(2,1)}, f32[2,3,2,8,2,16,128]{6,5,4,3,2,1,0:T(8,128)S(1)}) custom-call(s32[2]{0:T(128)S(1)} %pad_add_fusion.places, s32[16]{0:T(128)S(1)} %copy-done, bf16[8,32,16,128]{3,2,1,0:T(8,128)(2,1)S(1)} %all-to-all-done.1.moved, bf16[3,2,8,2,16,128]{5,4,3,2,1,0:T(8,128)(2,1)S(1)} %pad_maximum_fusion.1.same_core, ...), custom_call_target="tpu_custom_call" | custom-call | flops 3623878656 | bytes 2883584 | tf_op jit(solution)/shard_map/attention/pallas_call | solution.py:208
  55.0 0.1 fusion
  55.1 2.3 %collective-permute-start.3 = (bf16[3,2,8,2,16,128]{5,4,3,2,1,0:T(8,128)(2,1)S(1)}, bf16[3,2,8,2,16,128]{5,4,3,2,1,0:T(8,128)(2,1)S(1)}, u32[]{:S(2)}, u32[]{:S(2)}) collective-permute-start(bf16[3,2,8,2,16,128]{5,4,3,2,1,0:T(8,128)(2,1)S(1)} %fusion), channel_id=1, source_target_pairs={{0,8},{8,0},{1,9},{9,1},{2,10},{10,2},{3,11},{11,3},{4,12},{12,4},... | collective-permute-start | bytes 1179656 | tf_op jit(solution)/shard_map/ppermute | solution.py:293
  57.4 5.1 %all-to-all-start.2 = ((bf16[8,32,16,128]{3,2,1,0:T(8,128)(2,1)}), bf16[8,32,16,128]{3,2,1,0:T(8,128)(2,1)S(1)}, u32[]{:S(2)}, u32[]{:S(2)}) async-start(bf16[8,32,16,128]{3,2,1,0:T(8,128)(2,1)} %get-tuple-element.16), calls=%async_computation.2 | async-start | bytes 2097152 | tf_op jit(solution)/shard_map/all_to_all | solution.py:297
  62.4 0.0 collective-permute-done.3
  62.4 0.2 fusion.4
  62.6 3.2 %collective-permute-start.4 = (bf16[2,8,2,16,128]{4,3,2,1,0:T(8,128)(2,1)S(1)}, bf16[2,8,2,16,128]{4,3,2,1,0:T(8,128)(2,1)S(1)}, u32[]{:S(2)}, u32[]{:S(2)}) collective-permute-start(bf16[2,8,2,16,128]{4,3,2,1,0:T(8,128)(2,1)S(1)} %get-tuple-element.26), channel_id=1, source_target_pairs={{0,480},{32,0},{64,32},{96,64},{128,96},{160,128},{192,160},{224,1... | collective-permute-start | bytes 393224 | tf_op jit(solution)/shard_map/ppermute | solution.py:293
  65.9 4.4 %collective-permute-start.5 = (bf16[2,8,2,16,128]{4,3,2,1,0:T(8,128)(2,1)S(1)}, bf16[2,8,2,16,128]{4,3,2,1,0:T(8,128)(2,1)S(1)}, u32[]{:S(2)}, u32[]{:S(2)}) collective-permute-start(bf16[2,8,2,16,128]{4,3,2,1,0:T(8,128)(2,1)S(1)} %get-tuple-element.27), channel_id=1, source_target_pairs={{0,448},{32,480},{64,0},{96,32},{128,64},{160,96},{192,128},{224,1... | collective-permute-start | bytes 393224 | tf_op jit(solution)/shard_map/ppermute | solution.py:293
  70.3 0.0 collective-permute-done.4
  70.3 5.7 %collective-permute-done.5 = bf16[2,8,2,16,128]{4,3,2,1,0:T(8,128)(2,1)S(1)} collective-permute-done((bf16[2,8,2,16,128]{4,3,2,1,0:T(8,128)(2,1)S(1)}, bf16[2,8,2,16,128]{4,3,2,1,0:T(8,128)(2,1)S(1)}, u32[]{:S(2)}, u32[]{:S(2)}) %collective-permute-start.5) | collective-permute-done | bytes 131104 | tf_op jit(solution)/shard_map/ppermute | solution.py:293
  76.0 0.7 fusion.3
  76.7 1.6 %all-to-all-done.2.back = bf16[8,32,16,128]{3,2,1,0:T(8,128)(2,1)S(1)} async-done(((bf16[8,32,16,128]{3,2,1,0:T(8,128)(2,1)}), bf16[8,32,16,128]{3,2,1,0:T(8,128)(2,1)S(1)}, u32[]{:S(2)}, u32[]{:S(2)}) %all-to-all-start.2) | async-done | bytes 1048608 | tf_op jit(solution)/shard_map/all_to_all | solution.py:297
  78.3 3.5 %all-to-all-start.3 = ((bf16[16,2,16,128]{3,2,1,0:T(8,128)(2,1)}), bf16[16,2,16,128]{3,2,1,0:T(8,128)(2,1)S(1)}, u32[]{:S(2)}, u32[]{:S(2)}) async-start(bf16[16,2,16,128]{3,2,1,0:T(8,128)(2,1)} %bitcast.19), calls=%async_computation.3 | async-start | bytes 262144 | tf_op jit(solution)/shard_map/all_to_all | solution.py:302
  81.8 1.1 %spread.1 = (bf16[16,128,128]{2,1,0:T(8,128)(2,1)}, bf16[16,128,128]{2,1,0:T(8,128)(2,1)}) custom-call(bf16[8,32,16,128]{3,2,1,0:T(8,128)(2,1)S(1)} %all-to-all-done.2.back), custom_call_target="tpu_custom_call" | custom-call | tf_op jit(solution)/shard_map/spread/pallas_call | solution.py:258
  82.9 5.7 %all-to-all-done.3 = bf16[16,2,16,128]{3,2,1,0:T(8,128)(2,1)S(1)} async-done(((bf16[16,2,16,128]{3,2,1,0:T(8,128)(2,1)}), bf16[16,2,16,128]{3,2,1,0:T(8,128)(2,1)S(1)}, u32[]{:S(2)}, u32[]{:S(2)}) %all-to-all-start.3) | async-done | bytes 131104 | tf_op jit(solution)/shard_map/all_to_all | solution.py:302
  88.6 0.7 split.1
  (3 shorter events, 0.1 us)
Async XLA Ops:
  2.1 14.4 %all-to-all-start = ((bf16[16,2,16,128]{3,2,1,0:T(8,128)(2,1)}), bf16[16,2,16,128]{3,2,1,0:T(8,128)(2,1)S(1)}, u32[]{:S(2)}, u32[]{:S(2)}) async-start(bf16[16,2,16,128]{3,2,1,0:T(8,128)(2,1)} %bitcast.5), calls=%async_computation | async-start | bytes 262144 | tf_op jit(solution)/shard_map/all_to_all | solution.py:302
  12.2 32.4 %copy-start = (s32[16]{0:T(128)S(1)}, s32[16]{0:T(128)}, u32[]{:S(2)}) copy-start(s32[16]{0:T(128)} %lengths.1) | copy-start | bytes 196
  16.5 28.1 %all-to-all-start.1 = ((bf16[8,32,16,128]{3,2,1,0:T(8,128)(2,1)}), bf16[8,32,16,128]{3,2,1,0:T(8,128)(2,1)S(1)}, u32[]{:S(2)}, u32[]{:S(2)}) async-start(bf16[8,32,16,128]{3,2,1,0:T(8,128)(2,1)} %bitcast.35), calls=%async_computation.1 | async-start | bytes 2097152 | tf_op jit(solution)/shard_map/all_to_all | solution.py:297
  20.1 14.0 %collective-permute-start.1 = (bf16[2,8,2,16,128]{4,3,2,1,0:T(8,128)(2,1)S(1)}, bf16[2,8,2,16,128]{4,3,2,1,0:T(8,128)(2,1)S(1)}, u32[]{:S(2)}, u32[]{:S(2)}) collective-permute-start(bf16[2,8,2,16,128]{4,3,2,1,0:T(8,128)(2,1)S(1)} %bitcast.38), channel_id=1, source_target_pairs={{0,64},{32,96},{64,128},{96,160},{128,192},{160,224},{192,256},{22... | collective-permute-start | bytes 393224 | tf_op jit(solution)/shard_map/ppermute | solution.py:293
  25.0 15.0 %collective-permute-start = (bf16[2,8,2,16,128]{4,3,2,1,0:T(8,128)(2,1)S(1)}, bf16[2,8,2,16,128]{4,3,2,1,0:T(8,128)(2,1)S(1)}, u32[]{:S(2)}, u32[]{:S(2)}) collective-permute-start(bf16[2,8,2,16,128]{4,3,2,1,0:T(8,128)(2,1)S(1)} %bitcast.39), channel_id=1, source_target_pairs={{0,32},{32,64},{64,96},{96,128},{128,160},{160,192},{192,224},{224... | collective-permute-start | bytes 393224 | tf_op jit(solution)/shard_map/ppermute | solution.py:293
  40.0 4.6 %collective-permute-start.2 = (bf16[3,2,8,2,16,128]{5,4,3,2,1,0:T(8,128)(2,1)S(1)}, bf16[3,2,8,2,16,128]{5,4,3,2,1,0:T(8,128)(2,1)S(1)}, u32[]{:S(2)}, u32[]{:S(2)}) collective-permute-start(bf16[3,2,8,2,16,128]{5,4,3,2,1,0:T(8,128)(2,1)S(1)} %pad_maximum_fusion.1.same_core), channel_id=1, source_target_pairs={{0,8},{8,0},{1,9},{9,1},{2,10},{10,2},{3,11},{11,3},{4,12},{12,4},... | collective-permute-start | bytes 1179656 | tf_op jit(solution)/shard_map/ppermute | solution.py:293
  55.1 7.4 %collective-permute-start.3 = (bf16[3,2,8,2,16,128]{5,4,3,2,1,0:T(8,128)(2,1)S(1)}, bf16[3,2,8,2,16,128]{5,4,3,2,1,0:T(8,128)(2,1)S(1)}, u32[]{:S(2)}, u32[]{:S(2)}) collective-permute-start(bf16[3,2,8,2,16,128]{5,4,3,2,1,0:T(8,128)(2,1)S(1)} %fusion), channel_id=1, source_target_pairs={{0,8},{8,0},{1,9},{9,1},{2,10},{10,2},{3,11},{11,3},{4,12},{12,4},... | collective-permute-start | bytes 1179656 | tf_op jit(solution)/shard_map/ppermute | solution.py:293
  57.4 21.0 %all-to-all-start.2 = ((bf16[8,32,16,128]{3,2,1,0:T(8,128)(2,1)}), bf16[8,32,16,128]{3,2,1,0:T(8,128)(2,1)S(1)}, u32[]{:S(2)}, u32[]{:S(2)}) async-start(bf16[8,32,16,128]{3,2,1,0:T(8,128)(2,1)} %get-tuple-element.16), calls=%async_computation.2 | async-start | bytes 2097152 | tf_op jit(solution)/shard_map/all_to_all | solution.py:297
  62.6 7.6 %collective-permute-start.4 = (bf16[2,8,2,16,128]{4,3,2,1,0:T(8,128)(2,1)S(1)}, bf16[2,8,2,16,128]{4,3,2,1,0:T(8,128)(2,1)S(1)}, u32[]{:S(2)}, u32[]{:S(2)}) collective-permute-start(bf16[2,8,2,16,128]{4,3,2,1,0:T(8,128)(2,1)S(1)} %get-tuple-element.26), channel_id=1, source_target_pairs={{0,480},{32,0},{64,32},{96,64},{128,96},{160,128},{192,160},{224,1... | collective-permute-start | bytes 393224 | tf_op jit(solution)/shard_map/ppermute | solution.py:293
  65.9 10.1 %collective-permute-start.5 = (bf16[2,8,2,16,128]{4,3,2,1,0:T(8,128)(2,1)S(1)}, bf16[2,8,2,16,128]{4,3,2,1,0:T(8,128)(2,1)S(1)}, u32[]{:S(2)}, u32[]{:S(2)}) collective-permute-start(bf16[2,8,2,16,128]{4,3,2,1,0:T(8,128)(2,1)S(1)} %get-tuple-element.27), channel_id=1, source_target_pairs={{0,448},{32,480},{64,0},{96,32},{128,64},{160,96},{192,128},{224,1... | collective-permute-start | bytes 393224 | tf_op jit(solution)/shard_map/ppermute | solution.py:293
  78.3 10.3 %all-to-all-start.3 = ((bf16[16,2,16,128]{3,2,1,0:T(8,128)(2,1)}), bf16[16,2,16,128]{3,2,1,0:T(8,128)(2,1)S(1)}, u32[]{:S(2)}, u32[]{:S(2)}) async-start(bf16[16,2,16,128]{3,2,1,0:T(8,128)(2,1)} %bitcast.19), calls=%async_computation.3 | async-start | bytes 262144 | tf_op jit(solution)/shard_map/all_to_all | solution.py:302

commit v2 on v1

--- a/solution.py
+++ b/solution.py
@@ -116,7 +116,8 @@
         clear(weight_all, chunk)
         inverse = 1.0 / total
         state[chunk] = {
-            index: jnp.exp2((most - highest) * scale) * inverse for index, most in seen.items()
+            index: (jnp.exp2((most - highest) * scale) * inverse).astype(jnp.bfloat16)
+            for index, most in seen.items()
         }
 
     def backward(chunk):
@@ -124,8 +125,7 @@
         factors = state.pop(chunk)
         for index in range(REACH + 1):
             part = rows_of(index, chunk)
-            weights = weight_all[part, lanes_of(chunk)].astype(jnp.float32)
-            weight_all[part, lanes_of(chunk)] = (weights * factors[index]).astype(jnp.bfloat16)
+            weight_all[part, lanes_of(chunk)] = weight_all[part, lanes_of(chunk)] * factors[index]
             if index % 3 == 2:
                 yield
         attended = dot(values_t[...], weight_all[:, lanes_of(chunk)], ((1,), (0,)))
@@ -138,8 +138,8 @@
         for index in range(REACH + 1):
             part = rows_of(index, chunk)
             dprob = dot(values[part, :], grad, ((1,), (1,)))
-            weights = weight_all[part, lanes_of(chunk)].astype(jnp.float32)
-            dscore_all[part, lanes_of(chunk)] = (weights * (dprob - delta)).astype(jnp.bfloat16)
+            slope = (dprob - delta).astype(jnp.bfloat16)
+            dscore_all[part, lanes_of(chunk)] = weight_all[part, lanes_of(chunk)] * slope
             yield
         clear(dscore_all, chunk)
         query_grad = dot(keys_t[...], dscore_all[:, lanes_of(chunk)], ((1,), (0,))) * inv_root

time: 90.2 us -> 89.6 us (level)
  no operation moved by 1% of the time
where the time goes in v2:
time: 89.6 us; the launch traced here: 88.7 us
  starting transfers between devices  41.3 us (46%)
  waiting for transfers between devices  30.1 us (34%)
  Pallas kernels  11.5 us (13%)
  other arithmetic  3.08 us (3%)
  local copies, waits for them, and re-layouts  1.94 us (2%)
    ppermute x6, starting transfers between devices, turned(): lax.ppermute(block, axis, [(i, (i + distance) % size) for i in range(size)])  21.6 us
    ppermute x6, waiting for transfers between devices, turned(): lax.ppermute(block, axis, [(i, (i + distance) % size) for i in range(size)])  18.4 us
    all_to_all x2, starting transfers between devices, crossed(): lax.all_to_all(flat, ('yhi', 'head'), split_axis=0, concat_axis=0, tiled=...  11.1 us
    all_to_all x2, waiting for transfers between devices, crossed(): lax.all_to_all(flat, ('yhi', 'head'), split_axis=0, concat_axis=0, tiled=...  10.1 us
    pallas_call x1, Pallas kernels, attention(): pl.pallas_call(attention_kernel, out_shape=(jax.ShapeDtypeStruct(moved.sh...  9.75 us
    all_to_all x2, starting transfers between devices, swapped(): lax.all_to_all(block, 'head', split_axis=0, concat_axis=0, tiled=True)  8.63 us
  transfers between devices with their start and end apart: 10, of which 7 were waited for; matrix products, arithmetic and copies ran while one was open for 4% of the time, Pallas kernels for 1%

profile of v2, /device:TPU:1, one launch (start us, length us, event | category | flops | bytes accessed | tf_op | source)
XLA Modules:
  0.0 88.7 jit_solution(498095290470922539)
XLA Ops:
  0.6 0.8 maximum_bitcast_fusion
  1.4 0.7 broadcast_in_dim.2
  2.1 7.6 %all-to-all-start = ((bf16[16,2,16,128]{3,2,1,0:T(8,128)(2,1)}), bf16[16,2,16,128]{3,2,1,0:T(8,128)(2,1)S(1)}, u32[]{:S(2)}, u32[]{:S(2)}) async-start(bf16[16,2,16,128]{3,2,1,0:T(8,128)(2,1)} %bitcast.5), calls=%async_computation | async-start | bytes 262144 | tf_op jit(solution)/shard_map/all_to_all | solution.py:302
  9.7 1.3 %pad_maximum_fusion = bf16[2,16,128,128]{3,2,1,0:T(8,128)(2,1)S(1)} fusion(bf16[1,16,128,128]{3,2,1,0:T(8,128)(2,1)} %bitcast.41, bf16[1,16,128,128]{3,2,1,0:T(8,128)(2,1)} %bitcast.42), kind=kLoop, calls=%fused_computation | loop fusion | flops 524288 | bytes 2097152 | tf_op jit(solution)/shard_map/stack | solution.py:313
  11.0 1.2 %copy.13 = bf16[32,8,16,128]{3,2,0,1:T(8,128)(2,1)} copy(bf16[32,8,16,128]{3,2,1,0:T(8,128)(2,1)S(1)} %bitcast.37) | data formatting | bytes 2097152 | tf_op jit(solution)/shard_map/reshape | solution.py:313
  12.2 0.0 copy-start
  12.2 4.4 %all-to-all-done = bf16[16,2,16,128]{3,2,1,0:T(8,128)(2,1)S(1)} async-done(((bf16[16,2,16,128]{3,2,1,0:T(8,128)(2,1)}), bf16[16,2,16,128]{3,2,1,0:T(8,128)(2,1)S(1)}, u32[]{:S(2)}, u32[]{:S(2)}) %all-to-all-start) | async-done | bytes 131104 | tf_op jit(solution)/shard_map/all_to_all | solution.py:302
  16.5 3.6 %all-to-all-start.1 = ((bf16[8,32,16,128]{3,2,1,0:T(8,128)(2,1)}), bf16[8,32,16,128]{3,2,1,0:T(8,128)(2,1)S(1)}, u32[]{:S(2)}, u32[]{:S(2)}) async-start(bf16[8,32,16,128]{3,2,1,0:T(8,128)(2,1)} %bitcast.35), calls=%async_computation.1 | async-start | bytes 2097152 | tf_op jit(solution)/shard_map/all_to_all | solution.py:297
  20.1 4.9 %collective-permute-start.1 = (bf16[2,8,2,16,128]{4,3,2,1,0:T(8,128)(2,1)S(1)}, bf16[2,8,2,16,128]{4,3,2,1,0:T(8,128)(2,1)S(1)}, u32[]{:S(2)}, u32[]{:S(2)}) collective-permute-start(bf16[2,8,2,16,128]{4,3,2,1,0:T(8,128)(2,1)S(1)} %bitcast.38), channel_id=1, source_target_pairs={{0,64},{32,96},{64,128},{96,160},{128,192},{160,224},{192,256},{22... | collective-permute-start | bytes 393224 | tf_op jit(solution)/shard_map/ppermute | solution.py:293
  25.0 3.5 %collective-permute-start = (bf16[2,8,2,16,128]{4,3,2,1,0:T(8,128)(2,1)S(1)}, bf16[2,8,2,16,128]{4,3,2,1,0:T(8,128)(2,1)S(1)}, u32[]{:S(2)}, u32[]{:S(2)}) collective-permute-start(bf16[2,8,2,16,128]{4,3,2,1,0:T(8,128)(2,1)S(1)} %bitcast.39), channel_id=1, source_target_pairs={{0,32},{32,64},{64,96},{96,128},{128,160},{160,192},{192,224},{224... | collective-permute-start | bytes 393224 | tf_op jit(solution)/shard_map/ppermute | solution.py:293
  28.6 5.6 %collective-permute-done.1 = bf16[2,8,2,16,128]{4,3,2,1,0:T(8,128)(2,1)S(1)} collective-permute-done((bf16[2,8,2,16,128]{4,3,2,1,0:T(8,128)(2,1)S(1)}, bf16[2,8,2,16,128]{4,3,2,1,0:T(8,128)(2,1)S(1)}, u32[]{:S(2)}, u32[]{:S(2)}) %collective-permute-start.1) | collective-permute-done | bytes 131104 | tf_op jit(solution)/shard_map/ppermute | solution.py:293
  34.1 5.9 %collective-permute-done = bf16[2,8,2,16,128]{4,3,2,1,0:T(8,128)(2,1)S(1)} collective-permute-done((bf16[2,8,2,16,128]{4,3,2,1,0:T(8,128)(2,1)S(1)}, bf16[2,8,2,16,128]{4,3,2,1,0:T(8,128)(2,1)S(1)}, u32[]{:S(2)}, u32[]{:S(2)}) %collective-permute-start) | collective-permute-done | bytes 131104 | tf_op jit(solution)/shard_map/ppermute | solution.py:293
  40.0 3.2 %collective-permute-start.2 = (bf16[3,2,8,2,16,128]{5,4,3,2,1,0:T(8,128)(2,1)S(1)}, bf16[3,2,8,2,16,128]{5,4,3,2,1,0:T(8,128)(2,1)S(1)}, u32[]{:S(2)}, u32[]{:S(2)}) collective-permute-start(bf16[3,2,8,2,16,128]{5,4,3,2,1,0:T(8,128)(2,1)S(1)} %pad_maximum_fusion.1.same_core), channel_id=1, source_target_pairs={{0,8},{8,0},{1,9},{9,1},{2,10},{10,2},{3,11},{11,3},{4,12},{12,4},... | collective-permute-start | bytes 1179656 | tf_op jit(solution)/shard_map/ppermute | solution.py:293
  43.3 0.1 pad_add_fusion.places
  43.4 1.2 %collective-permute-done.2.other_core = bf16[3,2,8,2,16,128]{5,4,3,2,1,0:T(8,128)(2,1)S(1)} collective-permute-done((bf16[3,2,8,2,16,128]{5,4,3,2,1,0:T(8,128)(2,1)S(1)}, bf16[3,2,8,2,16,128]{5,4,3,2,1,0:T(8,128)(2,1)S(1)}, u32[]{:S(2)}, u32[]{:S(2)}) %collective-permute-start.2) | collective-permute-done | bytes 393248 | tf_op jit(solution)/shard_map/ppermute | solution.py:293
  44.6 0.0 all-to-all-done.1.moved
  44.6 0.0 copy-done
  44.6 9.7 %attention.1 = (bf16[8,32,16,128]{3,2,1,0:T(8,128)(2,1)}, f32[2,3,2,8,2,16,128]{6,5,4,3,2,1,0:T(8,128)S(1)}) custom-call(s32[2]{0:T(128)S(1)} %pad_add_fusion.places, s32[16]{0:T(128)S(1)} %copy-done, bf16[8,32,16,128]{3,2,1,0:T(8,128)(2,1)S(1)} %all-to-all-done.1.moved, bf16[3,2,8,2,16,128]{5,4,3,2,1,0:T(8,128)(2,1)S(1)} %pad_maximum_fusion.1.same_core, ...), custom_call_target="tpu_custom_call" | custom-call | flops 3623878656 | bytes 2883584 | tf_op jit(solution)/shard_map/attention/pallas_call | solution.py:208
  54.4 0.1 fusion
  54.4 2.3 %collective-permute-start.3 = (bf16[3,2,8,2,16,128]{5,4,3,2,1,0:T(8,128)(2,1)S(1)}, bf16[3,2,8,2,16,128]{5,4,3,2,1,0:T(8,128)(2,1)S(1)}, u32[]{:S(2)}, u32[]{:S(2)}) collective-permute-start(bf16[3,2,8,2,16,128]{5,4,3,2,1,0:T(8,128)(2,1)S(1)} %fusion), channel_id=1, source_target_pairs={{0,8},{8,0},{1,9},{9,1},{2,10},{10,2},{3,11},{11,3},{4,12},{12,4},... | collective-permute-start | bytes 1179656 | tf_op jit(solution)/shard_map/ppermute | solution.py:293
  56.7 5.1 %all-to-all-start.2 = ((bf16[8,32,16,128]{3,2,1,0:T(8,128)(2,1)}), bf16[8,32,16,128]{3,2,1,0:T(8,128)(2,1)S(1)}, u32[]{:S(2)}, u32[]{:S(2)}) async-start(bf16[8,32,16,128]{3,2,1,0:T(8,128)(2,1)} %get-tuple-element.16), calls=%async_computation.2 | async-start | bytes 2097152 | tf_op jit(solution)/shard_map/all_to_all | solution.py:297
  61.8 0.0 collective-permute-done.3
  61.8 0.2 fusion.4
  62.0 3.2 %collective-permute-start.4 = (bf16[2,8,2,16,128]{4,3,2,1,0:T(8,128)(2,1)S(1)}, bf16[2,8,2,16,128]{4,3,2,1,0:T(8,128)(2,1)S(1)}, u32[]{:S(2)}, u32[]{:S(2)}) collective-permute-start(bf16[2,8,2,16,128]{4,3,2,1,0:T(8,128)(2,1)S(1)} %get-tuple-element.26), channel_id=1, source_target_pairs={{0,480},{32,0},{64,32},{96,64},{128,96},{160,128},{192,160},{224,1... | collective-permute-start | bytes 393224 | tf_op jit(solution)/shard_map/ppermute | solution.py:293
  65.2 4.4 %collective-permute-start.5 = (bf16[2,8,2,16,128]{4,3,2,1,0:T(8,128)(2,1)S(1)}, bf16[2,8,2,16,128]{4,3,2,1,0:T(8,128)(2,1)S(1)}, u32[]{:S(2)}, u32[]{:S(2)}) collective-permute-start(bf16[2,8,2,16,128]{4,3,2,1,0:T(8,128)(2,1)S(1)} %get-tuple-element.27), channel_id=1, source_target_pairs={{0,448},{32,480},{64,0},{96,32},{128,64},{160,96},{192,128},{224,1... | collective-permute-start | bytes 393224 | tf_op jit(solution)/shard_map/ppermute | solution.py:293
  69.6 0.0 collective-permute-done.4
  69.6 5.8 %collective-permute-done.5 = bf16[2,8,2,16,128]{4,3,2,1,0:T(8,128)(2,1)S(1)} collective-permute-done((bf16[2,8,2,16,128]{4,3,2,1,0:T(8,128)(2,1)S(1)}, bf16[2,8,2,16,128]{4,3,2,1,0:T(8,128)(2,1)S(1)}, u32[]{:S(2)}, u32[]{:S(2)}) %collective-permute-start.5) | collective-permute-done | bytes 131104 | tf_op jit(solution)/shard_map/ppermute | solution.py:293
  75.4 0.7 fusion.3
  76.1 1.6 %all-to-all-done.2.back = bf16[8,32,16,128]{3,2,1,0:T(8,128)(2,1)S(1)} async-done(((bf16[8,32,16,128]{3,2,1,0:T(8,128)(2,1)}), bf16[8,32,16,128]{3,2,1,0:T(8,128)(2,1)S(1)}, u32[]{:S(2)}, u32[]{:S(2)}) %all-to-all-start.2) | async-done | bytes 1048608 | tf_op jit(solution)/shard_map/all_to_all | solution.py:297
  77.7 3.5 %all-to-all-start.3 = ((bf16[16,2,16,128]{3,2,1,0:T(8,128)(2,1)}), bf16[16,2,16,128]{3,2,1,0:T(8,128)(2,1)S(1)}, u32[]{:S(2)}, u32[]{:S(2)}) async-start(bf16[16,2,16,128]{3,2,1,0:T(8,128)(2,1)} %bitcast.19), calls=%async_computation.3 | async-start | bytes 262144 | tf_op jit(solution)/shard_map/all_to_all | solution.py:302
  81.2 1.1 %spread.1 = (bf16[16,128,128]{2,1,0:T(8,128)(2,1)}, bf16[16,128,128]{2,1,0:T(8,128)(2,1)}) custom-call(bf16[8,32,16,128]{3,2,1,0:T(8,128)(2,1)S(1)} %all-to-all-done.2.back), custom_call_target="tpu_custom_call" | custom-call | tf_op jit(solution)/shard_map/spread/pallas_call | solution.py:258
  82.3 5.7 %all-to-all-done.3 = bf16[16,2,16,128]{3,2,1,0:T(8,128)(2,1)S(1)} async-done(((bf16[16,2,16,128]{3,2,1,0:T(8,128)(2,1)}), bf16[16,2,16,128]{3,2,1,0:T(8,128)(2,1)S(1)}, u32[]{:S(2)}, u32[]{:S(2)}) %all-to-all-start.3) | async-done | bytes 131104 | tf_op jit(solution)/shard_map/all_to_all | solution.py:302
  88.0 0.7 split.1
  (3 shorter events, 0.1 us)
Async XLA Ops:
  2.1 14.4 %all-to-all-start = ((bf16[16,2,16,128]{3,2,1,0:T(8,128)(2,1)}), bf16[16,2,16,128]{3,2,1,0:T(8,128)(2,1)S(1)}, u32[]{:S(2)}, u32[]{:S(2)}) async-start(bf16[16,2,16,128]{3,2,1,0:T(8,128)(2,1)} %bitcast.5), calls=%async_computation | async-start | bytes 262144 | tf_op jit(solution)/shard_map/all_to_all | solution.py:302
  12.2 32.4 %copy-start = (s32[16]{0:T(128)S(1)}, s32[16]{0:T(128)}, u32[]{:S(2)}) copy-start(s32[16]{0:T(128)} %lengths.1) | copy-start | bytes 196
  16.5 28.1 %all-to-all-start.1 = ((bf16[8,32,16,128]{3,2,1,0:T(8,128)(2,1)}), bf16[8,32,16,128]{3,2,1,0:T(8,128)(2,1)S(1)}, u32[]{:S(2)}, u32[]{:S(2)}) async-start(bf16[8,32,16,128]{3,2,1,0:T(8,128)(2,1)} %bitcast.35), calls=%async_computation.1 | async-start | bytes 2097152 | tf_op jit(solution)/shard_map/all_to_all | solution.py:297
  20.1 14.0 %collective-permute-start.1 = (bf16[2,8,2,16,128]{4,3,2,1,0:T(8,128)(2,1)S(1)}, bf16[2,8,2,16,128]{4,3,2,1,0:T(8,128)(2,1)S(1)}, u32[]{:S(2)}, u32[]{:S(2)}) collective-permute-start(bf16[2,8,2,16,128]{4,3,2,1,0:T(8,128)(2,1)S(1)} %bitcast.38), channel_id=1, source_target_pairs={{0,64},{32,96},{64,128},{96,160},{128,192},{160,224},{192,256},{22... | collective-permute-start | bytes 393224 | tf_op jit(solution)/shard_map/ppermute | solution.py:293
  25.0 15.0 %collective-permute-start = (bf16[2,8,2,16,128]{4,3,2,1,0:T(8,128)(2,1)S(1)}, bf16[2,8,2,16,128]{4,3,2,1,0:T(8,128)(2,1)S(1)}, u32[]{:S(2)}, u32[]{:S(2)}) collective-permute-start(bf16[2,8,2,16,128]{4,3,2,1,0:T(8,128)(2,1)S(1)} %bitcast.39), channel_id=1, source_target_pairs={{0,32},{32,64},{64,96},{96,128},{128,160},{160,192},{192,224},{224... | collective-permute-start | bytes 393224 | tf_op jit(solution)/shard_map/ppermute | solution.py:293
  40.0 4.6 %collective-permute-start.2 = (bf16[3,2,8,2,16,128]{5,4,3,2,1,0:T(8,128)(2,1)S(1)}, bf16[3,2,8,2,16,128]{5,4,3,2,1,0:T(8,128)(2,1)S(1)}, u32[]{:S(2)}, u32[]{:S(2)}) collective-permute-start(bf16[3,2,8,2,16,128]{5,4,3,2,1,0:T(8,128)(2,1)S(1)} %pad_maximum_fusion.1.same_core), channel_id=1, source_target_pairs={{0,8},{8,0},{1,9},{9,1},{2,10},{10,2},{3,11},{11,3},{4,12},{12,4},... | collective-permute-start | bytes 1179656 | tf_op jit(solution)/shard_map/ppermute | solution.py:293
  54.4 7.4 %collective-permute-start.3 = (bf16[3,2,8,2,16,128]{5,4,3,2,1,0:T(8,128)(2,1)S(1)}, bf16[3,2,8,2,16,128]{5,4,3,2,1,0:T(8,128)(2,1)S(1)}, u32[]{:S(2)}, u32[]{:S(2)}) collective-permute-start(bf16[3,2,8,2,16,128]{5,4,3,2,1,0:T(8,128)(2,1)S(1)} %fusion), channel_id=1, source_target_pairs={{0,8},{8,0},{1,9},{9,1},{2,10},{10,2},{3,11},{11,3},{4,12},{12,4},... | collective-permute-start | bytes 1179656 | tf_op jit(solution)/shard_map/ppermute | solution.py:293
  56.7 21.0 %all-to-all-start.2 = ((bf16[8,32,16,128]{3,2,1,0:T(8,128)(2,1)}), bf16[8,32,16,128]{3,2,1,0:T(8,128)(2,1)S(1)}, u32[]{:S(2)}, u32[]{:S(2)}) async-start(bf16[8,32,16,128]{3,2,1,0:T(8,128)(2,1)} %get-tuple-element.16), calls=%async_computation.2 | async-start | bytes 2097152 | tf_op jit(solution)/shard_map/all_to_all | solution.py:297
  62.0 7.6 %collective-permute-start.4 = (bf16[2,8,2,16,128]{4,3,2,1,0:T(8,128)(2,1)S(1)}, bf16[2,8,2,16,128]{4,3,2,1,0:T(8,128)(2,1)S(1)}, u32[]{:S(2)}, u32[]{:S(2)}) collective-permute-start(bf16[2,8,2,16,128]{4,3,2,1,0:T(8,128)(2,1)S(1)} %get-tuple-element.26), channel_id=1, source_target_pairs={{0,480},{32,0},{64,32},{96,64},{128,96},{160,128},{192,160},{224,1... | collective-permute-start | bytes 393224 | tf_op jit(solution)/shard_map/ppermute | solution.py:293
  65.2 10.1 %collective-permute-start.5 = (bf16[2,8,2,16,128]{4,3,2,1,0:T(8,128)(2,1)S(1)}, bf16[2,8,2,16,128]{4,3,2,1,0:T(8,128)(2,1)S(1)}, u32[]{:S(2)}, u32[]{:S(2)}) collective-permute-start(bf16[2,8,2,16,128]{4,3,2,1,0:T(8,128)(2,1)S(1)} %get-tuple-element.27), channel_id=1, source_target_pairs={{0,448},{32,480},{64,0},{96,32},{128,64},{160,96},{192,128},{224,1... | collective-permute-start | bytes 393224 | tf_op jit(solution)/shard_map/ppermute | solution.py:293
  77.7 10.3 %all-to-all-start.3 = ((bf16[16,2,16,128]{3,2,1,0:T(8,128)(2,1)}), bf16[16,2,16,128]{3,2,1,0:T(8,128)(2,1)S(1)}, u32[]{:S(2)}, u32[]{:S(2)}) async-start(bf16[16,2,16,128]{3,2,1,0:T(8,128)(2,1)} %bitcast.19), calls=%async_computation.3 | async-start | bytes 262144 | tf_op jit(solution)/shard_map/all_to_all | solution.py:302

commit v3 on v2

--- a/solution.py
+++ b/solution.py
@@ -19,7 +19,7 @@
 
 def attention_kernel(
     places, lengths, moved, same_core, other_core, out_moved, out_window,
-    keys, values, keys_t, values_t, key_sum, value_sum, weight_all, dscore_all,
+    keys, values, keys_t, values_t, key_sum, value_sum, weight_all, dscore_all, ready, sems,
 ):
     chunks, _, group, width = moved.shape
     chunk_tok = moved.shape[1] // 2
@@ -87,6 +87,9 @@
             held[pl.ds(span - after, after), lanes_of(chunk)] = jnp.zeros((after, rows), held.dtype)
 
     state = {}
+
+    def leaving(chunk):
+        return pltpu.make_async_copy(ready.at[chunk], out_moved.at[chunk], sems.at[chunk])
 
     def forward(chunk):
         query, _ = operands(chunk)
@@ -130,7 +133,7 @@
                 yield
         attended = dot(values_t[...], weight_all[:, lanes_of(chunk)], ((1,), (0,)))
         attended = attended.astype(jnp.bfloat16)
-        out_moved[chunk, :chunk_tok] = attended.T.reshape(chunk_tok, group, width)
+        ready[chunk, :chunk_tok] = attended.T.reshape(chunk_tok, group, width)
         delta = jnp.sum(
             grad.T.astype(jnp.float32) * attended.astype(jnp.float32), axis=0, keepdims=True
         )
@@ -144,7 +147,8 @@
         clear(dscore_all, chunk)
         query_grad = dot(keys_t[...], dscore_all[:, lanes_of(chunk)], ((1,), (0,))) * inv_root
         query_grad = query_grad.astype(jnp.bfloat16)
-        out_moved[chunk, chunk_tok : 2 * chunk_tok] = query_grad.T.reshape(chunk_tok, group, width)
+        ready[chunk, chunk_tok:] = query_grad.T.reshape(chunk_tok, group, width)
+        leaving(chunk).start()
         yield
 
     def gather(first, count):
@@ -153,7 +157,16 @@
         query = moved[chosen, :chunk_tok].reshape(count * rows, width)
         grad = moved[chosen, chunk_tok:].reshape(count * rows, width)
         for index in range(REACH + 1):
-            part = part_of(index)
+            low, high = index * block, (index + 1) * block
+            if index == 0:
+                low = first * chunk_tok
+            if index == REACH:
+                high = low + (first + count) * chunk_tok
+                if not first:
+                    rest = pl.ds(high, span - high)
+                    value_sum[rest, :] = jnp.zeros((span - high, width), jnp.float32)
+                    key_sum[rest, :] = jnp.zeros((span - high, width), jnp.float32)
+            part = pl.ds(low, high - low)
             value_part = dot(weight_all[part, lanes], grad, ((1,), (0,)))
             key_part = dot(dscore_all[part, lanes], query, ((1,), (0,)))
             if first:
@@ -196,6 +209,8 @@
             out_window[away, plane, side, :, 1] = value_sum[part, :].reshape(shape)
         else:
             out_window[away, plane, side] = blank
+    for chunk in range(chunks):
+        leaving(chunk).wait()
 
 
 def attention(places, lengths, moved, same_core, other_core):
@@ -212,7 +227,7 @@
             jax.ShapeDtypeStruct((CORES,) + same_core.shape, jnp.float32),
         ),
         in_specs=[smem, smem, vmem, vmem, vmem],
-        out_specs=(vmem, vmem),
+        out_specs=(pl.BlockSpec(memory_space=pl.ANY), vmem),
         scratch_shapes=[
             pltpu.VMEM((span, width), jnp.bfloat16),
             pltpu.VMEM((span, width), jnp.bfloat16),
@@ -222,6 +237,8 @@
             pltpu.VMEM((span, width), jnp.float32),
             pltpu.VMEM((span, block * group), jnp.bfloat16),
             pltpu.VMEM((span, block * group), jnp.bfloat16),
+            pltpu.VMEM(moved.shape, jnp.bfloat16),
+            pltpu.SemaphoreType.DMA((chunks,)),
         ],
         compiler_params=pltpu.CompilerParams(vmem_limit_bytes=40 * 1024 * 1024),
         cost_estimate=pl.CostEstimate(
@@ -326,7 +343,7 @@
     beside = turned(out_window[1].astype(jnp.bfloat16), "core", 1)
     own = out_window[0] + beside.astype(jnp.float32)
     total = own[SPANS - 1]
-    for distance in range(1, SPANS):
+    for distance in range(SPANS - 1, 0, -1):
         sent = turned(own[SPANS - 1 - distance].astype(jnp.bfloat16), "z", -distance)
         total = total + sent.astype(jnp.float32)
     back, total = lax.optimization_barrier((back, total.astype(jnp.bfloat16)))

time: 89.6 us -> 89.4 us (level)
  transfers between devices with their start and end apart: 10 -> 10, of which waited for: 7 -> 8; matrix products, arithmetic and copies ran while one was open for 4% -> 4% of each run, Pallas kernels for 1% -> 1%
where the time goes in v3:
time: 89.4 us; the launch traced here: 88.6 us
  starting transfers between devices  41.3 us (46%)
  waiting for transfers between devices  30.1 us (34%)
  Pallas kernels  11.4 us (13%)
  other arithmetic  3.08 us (3%)
  local copies, waits for them, and re-layouts  1.94 us (2%)
    ppermute x6, starting transfers between devices, turned(): lax.ppermute(block, axis, [(i, (i + distance) % size) for i in range(size)])  21.6 us
    ppermute x6, waiting for transfers between devices, turned(): lax.ppermute(block, axis, [(i, (i + distance) % size) for i in range(size)])  18.4 us
    all_to_all x2, starting transfers between devices, crossed(): lax.all_to_all(flat, ('yhi', 'head'), split_axis=0, concat_axis=0, tiled=...  11.1 us
    all_to_all x2, waiting for transfers between devices, crossed(): lax.all_to_all(flat, ('yhi', 'head'), split_axis=0, concat_axis=0, tiled=...  10.1 us
    pallas_call x1, Pallas kernels, attention(): pl.pallas_call(attention_kernel, out_shape=(jax.ShapeDtypeStruct(moved.sh...  9.64 us
    all_to_all x2, starting transfers between devices, swapped(): lax.all_to_all(block, 'head', split_axis=0, concat_axis=0, tiled=True)  8.63 us
  transfers between devices with their start and end apart: 10, of which 8 were waited for; matrix products, arithmetic and copies ran while one was open for 4% of the time, Pallas kernels for 1%

profile of v3, /device:TPU:1, one launch (start us, length us, event | category | flops | bytes accessed | tf_op | source)
XLA Modules:
  0.0 88.6 jit_solution(5646748594389822637)
XLA Ops:
  0.6 0.8 maximum_bitcast_fusion
  1.4 0.7 broadcast_in_dim.2
  2.1 7.6 %all-to-all-start = ((bf16[16,2,16,128]{3,2,1,0:T(8,128)(2,1)}), bf16[16,2,16,128]{3,2,1,0:T(8,128)(2,1)S(1)}, u32[]{:S(2)}, u32[]{:S(2)}) async-start(bf16[16,2,16,128]{3,2,1,0:T(8,128)(2,1)} %bitcast.5), calls=%async_computation | async-start | bytes 262144 | tf_op jit(solution)/shard_map/all_to_all | solution.py:319
  9.7 1.3 %pad_maximum_fusion = bf16[2,16,128,128]{3,2,1,0:T(8,128)(2,1)S(1)} fusion(bf16[1,16,128,128]{3,2,1,0:T(8,128)(2,1)} %bitcast.41, bf16[1,16,128,128]{3,2,1,0:T(8,128)(2,1)} %bitcast.42), kind=kLoop, calls=%fused_computation | loop fusion | flops 524288 | bytes 2097152 | tf_op jit(solution)/shard_map/stack | solution.py:330
  11.0 1.2 %copy.13 = bf16[32,8,16,128]{3,2,0,1:T(8,128)(2,1)} copy(bf16[32,8,16,128]{3,2,1,0:T(8,128)(2,1)S(1)} %bitcast.37) | data formatting | bytes 2097152 | tf_op jit(solution)/shard_map/reshape | solution.py:330
  12.2 0.0 copy-start
  12.2 4.4 %all-to-all-done = bf16[16,2,16,128]{3,2,1,0:T(8,128)(2,1)S(1)} async-done(((bf16[16,2,16,128]{3,2,1,0:T(8,128)(2,1)}), bf16[16,2,16,128]{3,2,1,0:T(8,128)(2,1)S(1)}, u32[]{:S(2)}, u32[]{:S(2)}) %all-to-all-start) | async-done | bytes 131104 | tf_op jit(solution)/shard_map/all_to_all | solution.py:319
  16.5 3.6 %all-to-all-start.1 = ((bf16[8,32,16,128]{3,2,1,0:T(8,128)(2,1)}), bf16[8,32,16,128]{3,2,1,0:T(8,128)(2,1)S(1)}, u32[]{:S(2)}, u32[]{:S(2)}) async-start(bf16[8,32,16,128]{3,2,1,0:T(8,128)(2,1)} %bitcast.35), calls=%async_computation.1 | async-start | bytes 2097152 | tf_op jit(solution)/shard_map/all_to_all | solution.py:314
  20.1 4.9 %collective-permute-start.1 = (bf16[2,8,2,16,128]{4,3,2,1,0:T(8,128)(2,1)S(1)}, bf16[2,8,2,16,128]{4,3,2,1,0:T(8,128)(2,1)S(1)}, u32[]{:S(2)}, u32[]{:S(2)}) collective-permute-start(bf16[2,8,2,16,128]{4,3,2,1,0:T(8,128)(2,1)S(1)} %bitcast.38), channel_id=1, source_target_pairs={{0,64},{32,96},{64,128},{96,160},{128,192},{160,224},{192,256},{22... | collective-permute-start | bytes 393224 | tf_op jit(solution)/shard_map/ppermute | solution.py:310
  25.0 3.5 %collective-permute-start = (bf16[2,8,2,16,128]{4,3,2,1,0:T(8,128)(2,1)S(1)}, bf16[2,8,2,16,128]{4,3,2,1,0:T(8,128)(2,1)S(1)}, u32[]{:S(2)}, u32[]{:S(2)}) collective-permute-start(bf16[2,8,2,16,128]{4,3,2,1,0:T(8,128)(2,1)S(1)} %bitcast.39), channel_id=1, source_target_pairs={{0,32},{32,64},{64,96},{96,128},{128,160},{160,192},{192,224},{224... | collective-permute-start | bytes 393224 | tf_op jit(solution)/shard_map/ppermute | solution.py:310
  28.6 5.6 %collective-permute-done.1 = bf16[2,8,2,16,128]{4,3,2,1,0:T(8,128)(2,1)S(1)} collective-permute-done((bf16[2,8,2,16,128]{4,3,2,1,0:T(8,128)(2,1)S(1)}, bf16[2,8,2,16,128]{4,3,2,1,0:T(8,128)(2,1)S(1)}, u32[]{:S(2)}, u32[]{:S(2)}) %collective-permute-start.1) | collective-permute-done | bytes 131104 | tf_op jit(solution)/shard_map/ppermute | solution.py:310
  34.1 5.9 %collective-permute-done = bf16[2,8,2,16,128]{4,3,2,1,0:T(8,128)(2,1)S(1)} collective-permute-done((bf16[2,8,2,16,128]{4,3,2,1,0:T(8,128)(2,1)S(1)}, bf16[2,8,2,16,128]{4,3,2,1,0:T(8,128)(2,1)S(1)}, u32[]{:S(2)}, u32[]{:S(2)}) %collective-permute-start) | collective-permute-done | bytes 131104 | tf_op jit(solution)/shard_map/ppermute | solution.py:310
  40.0 3.2 %collective-permute-start.2 = (bf16[3,2,8,2,16,128]{5,4,3,2,1,0:T(8,128)(2,1)S(1)}, bf16[3,2,8,2,16,128]{5,4,3,2,1,0:T(8,128)(2,1)S(1)}, u32[]{:S(2)}, u32[]{:S(2)}) collective-permute-start(bf16[3,2,8,2,16,128]{5,4,3,2,1,0:T(8,128)(2,1)S(1)} %pad_maximum_fusion.1.same_core), channel_id=1, source_target_pairs={{0,8},{8,0},{1,9},{9,1},{2,10},{10,2},{3,11},{11,3},{4,12},{12,4},... | collective-permute-start | bytes 1179656 | tf_op jit(solution)/shard_map/ppermute | solution.py:310
  43.3 0.1 pad_add_fusion.places
  43.4 1.2 %collective-permute-done.2.other_core = bf16[3,2,8,2,16,128]{5,4,3,2,1,0:T(8,128)(2,1)S(1)} collective-permute-done((bf16[3,2,8,2,16,128]{5,4,3,2,1,0:T(8,128)(2,1)S(1)}, bf16[3,2,8,2,16,128]{5,4,3,2,1,0:T(8,128)(2,1)S(1)}, u32[]{:S(2)}, u32[]{:S(2)}) %collective-permute-start.2) | collective-permute-done | bytes 393248 | tf_op jit(solution)/shard_map/ppermute | solution.py:310
  44.6 0.0 all-to-all-done.1.moved
  44.6 0.0 copy-done
  44.6 9.6 %attention.1 = (bf16[8,32,16,128]{3,2,1,0:T(8,128)(2,1)}, f32[2,3,2,8,2,16,128]{6,5,4,3,2,1,0:T(8,128)S(1)}) custom-call(s32[2]{0:T(128)S(1)} %pad_add_fusion.places, s32[16]{0:T(128)S(1)} %copy-done, bf16[8,32,16,128]{3,2,1,0:T(8,128)(2,1)S(1)} %all-to-all-done.1.moved, bf16[3,2,8,2,16,128]{5,4,3,2,1,0:T(8,128)(2,1)S(1)} %pad_maximum_fusion.1.same_core, ...), custom_call_target="tpu_custom_call" | custom-call | flops 3623878656 | bytes 2883584 | tf_op jit(solution)/shard_map/attention/pallas_call | solution.py:223
  54.3 0.1 fusion
  54.3 2.3 %collective-permute-start.3 = (bf16[3,2,8,2,16,128]{5,4,3,2,1,0:T(8,128)(2,1)S(1)}, bf16[3,2,8,2,16,128]{5,4,3,2,1,0:T(8,128)(2,1)S(1)}, u32[]{:S(2)}, u32[]{:S(2)}) collective-permute-start(bf16[3,2,8,2,16,128]{5,4,3,2,1,0:T(8,128)(2,1)S(1)} %fusion), channel_id=1, source_target_pairs={{0,8},{8,0},{1,9},{9,1},{2,10},{10,2},{3,11},{11,3},{4,12},{12,4},... | collective-permute-start | bytes 1179656 | tf_op jit(solution)/shard_map/ppermute | solution.py:310
  56.6 5.1 %all-to-all-start.2 = ((bf16[8,32,16,128]{3,2,1,0:T(8,128)(2,1)}), bf16[8,32,16,128]{3,2,1,0:T(8,128)(2,1)S(1)}, u32[]{:S(2)}, u32[]{:S(2)}) async-start(bf16[8,32,16,128]{3,2,1,0:T(8,128)(2,1)} %get-tuple-element.16), calls=%async_computation.2 | async-start | bytes 2097152 | tf_op jit(solution)/shard_map/all_to_all | solution.py:314
  61.7 0.0 collective-permute-done.3
  61.7 0.2 fusion.4
  61.9 4.3 %collective-permute-start.4 = (bf16[2,8,2,16,128]{4,3,2,1,0:T(8,128)(2,1)S(1)}, bf16[2,8,2,16,128]{4,3,2,1,0:T(8,128)(2,1)S(1)}, u32[]{:S(2)}, u32[]{:S(2)}) collective-permute-start(bf16[2,8,2,16,128]{4,3,2,1,0:T(8,128)(2,1)S(1)} %get-tuple-element.26), channel_id=1, source_target_pairs={{0,448},{32,480},{64,0},{96,32},{128,64},{160,96},{192,128},{224,1... | collective-permute-start | bytes 393224 | tf_op jit(solution)/shard_map/ppermute | solution.py:310
  66.2 3.4 %collective-permute-start.5 = (bf16[2,8,2,16,128]{4,3,2,1,0:T(8,128)(2,1)S(1)}, bf16[2,8,2,16,128]{4,3,2,1,0:T(8,128)(2,1)S(1)}, u32[]{:S(2)}, u32[]{:S(2)}) collective-permute-start(bf16[2,8,2,16,128]{4,3,2,1,0:T(8,128)(2,1)S(1)} %get-tuple-element.27), channel_id=1, source_target_pairs={{0,480},{32,0},{64,32},{96,64},{128,96},{160,128},{192,160},{224,1... | collective-permute-start | bytes 393224 | tf_op jit(solution)/shard_map/ppermute | solution.py:310
  69.5 2.7 %collective-permute-done.4 = bf16[2,8,2,16,128]{4,3,2,1,0:T(8,128)(2,1)S(1)} collective-permute-done((bf16[2,8,2,16,128]{4,3,2,1,0:T(8,128)(2,1)S(1)}, bf16[2,8,2,16,128]{4,3,2,1,0:T(8,128)(2,1)S(1)}, u32[]{:S(2)}, u32[]{:S(2)}) %collective-permute-start.4) | collective-permute-done | bytes 131104 | tf_op jit(solution)/shard_map/ppermute | solution.py:310
  72.2 3.0 %collective-permute-done.5 = bf16[2,8,2,16,128]{4,3,2,1,0:T(8,128)(2,1)S(1)} collective-permute-done((bf16[2,8,2,16,128]{4,3,2,1,0:T(8,128)(2,1)S(1)}, bf16[2,8,2,16,128]{4,3,2,1,0:T(8,128)(2,1)S(1)}, u32[]{:S(2)}, u32[]{:S(2)}) %collective-permute-start.5) | collective-permute-done | bytes 131104 | tf_op jit(solution)/shard_map/ppermute | solution.py:310
  75.2 0.7 fusion.3
  76.0 1.6 %all-to-all-done.2.back = bf16[8,32,16,128]{3,2,1,0:T(8,128)(2,1)S(1)} async-done(((bf16[8,32,16,128]{3,2,1,0:T(8,128)(2,1)}), bf16[8,32,16,128]{3,2,1,0:T(8,128)(2,1)S(1)}, u32[]{:S(2)}, u32[]{:S(2)}) %all-to-all-start.2) | async-done | bytes 1048608 | tf_op jit(solution)/shard_map/all_to_all | solution.py:314
  77.6 3.5 %all-to-all-start.3 = ((bf16[16,2,16,128]{3,2,1,0:T(8,128)(2,1)}), bf16[16,2,16,128]{3,2,1,0:T(8,128)(2,1)S(1)}, u32[]{:S(2)}, u32[]{:S(2)}) async-start(bf16[16,2,16,128]{3,2,1,0:T(8,128)(2,1)} %bitcast.19), calls=%async_computation.3 | async-start | bytes 262144 | tf_op jit(solution)/shard_map/all_to_all | solution.py:319
  81.1 1.1 %spread.1 = (bf16[16,128,128]{2,1,0:T(8,128)(2,1)}, bf16[16,128,128]{2,1,0:T(8,128)(2,1)}) custom-call(bf16[8,32,16,128]{3,2,1,0:T(8,128)(2,1)S(1)} %all-to-all-done.2.back), custom_call_target="tpu_custom_call" | custom-call | tf_op jit(solution)/shard_map/spread/pallas_call | solution.py:275
  82.2 5.7 %all-to-all-done.3 = bf16[16,2,16,128]{3,2,1,0:T(8,128)(2,1)S(1)} async-done(((bf16[16,2,16,128]{3,2,1,0:T(8,128)(2,1)}), bf16[16,2,16,128]{3,2,1,0:T(8,128)(2,1)S(1)}, u32[]{:S(2)}, u32[]{:S(2)}) %all-to-all-start.3) | async-done | bytes 131104 | tf_op jit(solution)/shard_map/all_to_all | solution.py:319
  87.9 0.7 split.1
  (3 shorter events, 0.1 us)
Async XLA Ops:
  2.1 14.4 %all-to-all-start = ((bf16[16,2,16,128]{3,2,1,0:T(8,128)(2,1)}), bf16[16,2,16,128]{3,2,1,0:T(8,128)(2,1)S(1)}, u32[]{:S(2)}, u32[]{:S(2)}) async-start(bf16[16,2,16,128]{3,2,1,0:T(8,128)(2,1)} %bitcast.5), calls=%async_computation | async-start | bytes 262144 | tf_op jit(solution)/shard_map/all_to_all | solution.py:319
  12.2 32.4 %copy-start = (s32[16]{0:T(128)S(1)}, s32[16]{0:T(128)}, u32[]{:S(2)}) copy-start(s32[16]{0:T(128)} %lengths.1) | copy-start | bytes 196
  16.5 28.1 %all-to-all-start.1 = ((bf16[8,32,16,128]{3,2,1,0:T(8,128)(2,1)}), bf16[8,32,16,128]{3,2,1,0:T(8,128)(2,1)S(1)}, u32[]{:S(2)}, u32[]{:S(2)}) async-start(bf16[8,32,16,128]{3,2,1,0:T(8,128)(2,1)} %bitcast.35), calls=%async_computation.1 | async-start | bytes 2097152 | tf_op jit(solution)/shard_map/all_to_all | solution.py:314
  20.1 14.0 %collective-permute-start.1 = (bf16[2,8,2,16,128]{4,3,2,1,0:T(8,128)(2,1)S(1)}, bf16[2,8,2,16,128]{4,3,2,1,0:T(8,128)(2,1)S(1)}, u32[]{:S(2)}, u32[]{:S(2)}) collective-permute-start(bf16[2,8,2,16,128]{4,3,2,1,0:T(8,128)(2,1)S(1)} %bitcast.38), channel_id=1, source_target_pairs={{0,64},{32,96},{64,128},{96,160},{128,192},{160,224},{192,256},{22... | collective-permute-start | bytes 393224 | tf_op jit(solution)/shard_map/ppermute | solution.py:310
  25.0 15.0 %collective-permute-start = (bf16[2,8,2,16,128]{4,3,2,1,0:T(8,128)(2,1)S(1)}, bf16[2,8,2,16,128]{4,3,2,1,0:T(8,128)(2,1)S(1)}, u32[]{:S(2)}, u32[]{:S(2)}) collective-permute-start(bf16[2,8,2,16,128]{4,3,2,1,0:T(8,128)(2,1)S(1)} %bitcast.39), channel_id=1, source_target_pairs={{0,32},{32,64},{64,96},{96,128},{128,160},{160,192},{192,224},{224... | collective-permute-start | bytes 393224 | tf_op jit(solution)/shard_map/ppermute | solution.py:310
  40.0 4.6 %collective-permute-start.2 = (bf16[3,2,8,2,16,128]{5,4,3,2,1,0:T(8,128)(2,1)S(1)}, bf16[3,2,8,2,16,128]{5,4,3,2,1,0:T(8,128)(2,1)S(1)}, u32[]{:S(2)}, u32[]{:S(2)}) collective-permute-start(bf16[3,2,8,2,16,128]{5,4,3,2,1,0:T(8,128)(2,1)S(1)} %pad_maximum_fusion.1.same_core), channel_id=1, source_target_pairs={{0,8},{8,0},{1,9},{9,1},{2,10},{10,2},{3,11},{11,3},{4,12},{12,4},... | collective-permute-start | bytes 1179656 | tf_op jit(solution)/shard_map/ppermute | solution.py:310
  54.3 7.4 %collective-permute-start.3 = (bf16[3,2,8,2,16,128]{5,4,3,2,1,0:T(8,128)(2,1)S(1)}, bf16[3,2,8,2,16,128]{5,4,3,2,1,0:T(8,128)(2,1)S(1)}, u32[]{:S(2)}, u32[]{:S(2)}) collective-permute-start(bf16[3,2,8,2,16,128]{5,4,3,2,1,0:T(8,128)(2,1)S(1)} %fusion), channel_id=1, source_target_pairs={{0,8},{8,0},{1,9},{9,1},{2,10},{10,2},{3,11},{11,3},{4,12},{12,4},... | collective-permute-start | bytes 1179656 | tf_op jit(solution)/shard_map/ppermute | solution.py:310
  56.6 21.0 %all-to-all-start.2 = ((bf16[8,32,16,128]{3,2,1,0:T(8,128)(2,1)}), bf16[8,32,16,128]{3,2,1,0:T(8,128)(2,1)S(1)}, u32[]{:S(2)}, u32[]{:S(2)}) async-start(bf16[8,32,16,128]{3,2,1,0:T(8,128)(2,1)} %get-tuple-element.16), calls=%async_computation.2 | async-start | bytes 2097152 | tf_op jit(solution)/shard_map/all_to_all | solution.py:314
  61.9 10.3 %collective-permute-start.4 = (bf16[2,8,2,16,128]{4,3,2,1,0:T(8,128)(2,1)S(1)}, bf16[2,8,2,16,128]{4,3,2,1,0:T(8,128)(2,1)S(1)}, u32[]{:S(2)}, u32[]{:S(2)}) collective-permute-start(bf16[2,8,2,16,128]{4,3,2,1,0:T(8,128)(2,1)S(1)} %get-tuple-element.26), channel_id=1, source_target_pairs={{0,448},{32,480},{64,0},{96,32},{128,64},{160,96},{192,128},{224,1... | collective-permute-start | bytes 393224 | tf_op jit(solution)/shard_map/ppermute | solution.py:310
  66.2 9.1 %collective-permute-start.5 = (bf16[2,8,2,16,128]{4,3,2,1,0:T(8,128)(2,1)S(1)}, bf16[2,8,2,16,128]{4,3,2,1,0:T(8,128)(2,1)S(1)}, u32[]{:S(2)}, u32[]{:S(2)}) collective-permute-start(bf16[2,8,2,16,128]{4,3,2,1,0:T(8,128)(2,1)S(1)} %get-tuple-element.27), channel_id=1, source_target_pairs={{0,480},{32,0},{64,32},{96,64},{128,96},{160,128},{192,160},{224,1... | collective-permute-start | bytes 393224 | tf_op jit(solution)/shard_map/ppermute | solution.py:310
  77.6 10.3 %all-to-all-start.3 = ((bf16[16,2,16,128]{3,2,1,0:T(8,128)(2,1)}), bf16[16,2,16,128]{3,2,1,0:T(8,128)(2,1)S(1)}, u32[]{:S(2)}, u32[]{:S(2)}) async-start(bf16[16,2,16,128]{3,2,1,0:T(8,128)(2,1)} %bitcast.19), calls=%async_computation.3 | async-start | bytes 262144 | tf_op jit(solution)/shard_map/all_to_all | solution.py:319

commit v4 on v3

--- a/solution.py
+++ b/solution.py
@@ -305,6 +305,24 @@
     )(total)
 
 
+def held_kernel(block, out):
+    out[...] = block[...]
+
+
+def held(block):
+    vmem = pl.BlockSpec(memory_space=pltpu.VMEM)
+    return pl.pallas_call(
+        held_kernel,
+        out_shape=jax.ShapeDtypeStruct(block.shape, block.dtype),
+        in_specs=[vmem],
+        out_specs=vmem,
+        cost_estimate=pl.CostEstimate(
+            flops=5 * 10**9, bytes_accessed=4 * block.size, transcendentals=0
+        ),
+        name="held",
+    )(block)
+
+
 def turned(block, axis, distance):
     size = lax.axis_size(axis)
     return lax.ppermute(block, axis, [(i, (i + distance) % size) for i in range(size)])
@@ -332,6 +350,7 @@
     pair, both = lax.optimization_barrier((pair, both))
     moved = swapped(both)
     layers = [pair] + [turned(pair, "z", distance) for distance in range(1, SPANS)]
+    layers[-1] = held(layers[-1])
     same_core = jnp.stack(layers)
     other_core = turned(same_core, "core", 1)
 

time: 89.4 us -> 91 us (1.018)
  waiting for transfers between devices: 30.1 us -> 24.3 us
  starting transfers between devices: 41.3 us -> 45.7 us
  Pallas kernels: 11.4 us -> 13 us
    ppermute x6, waiting for transfers between devices: 18.4 us -> 12.3 us  [turned(): lax.ppermute(block, axis, [(i, (i + distance) % size) for i in range(size)])]
    ppermute x6, starting transfers between devices: 21.6 us -> 25.8 us  [turned(): lax.ppermute(block, axis, [(i, (i + distance) % size) for i in range(size)])]
    all_to_all x2, starting transfers between devices: 11.1 us -> 12.7 us  [crossed(): lax.all_to_all(flat, ('yhi', 'head'), split_axis=0, concat_axis=0, tiled=...]
    pallas_call x0 -> x1, Pallas kernels: none -> 1.57 us  [held(): pl.pallas_call(held_kernel, out_shape=jax.ShapeDtypeStruct(block.shape, b...]
    all_to_all x2, starting transfers between devices: 8.63 us -> 7.14 us  [swapped(): lax.all_to_all(block, 'head', split_axis=0, concat_axis=0, tiled=True)]
  transfers between devices with their start and end apart: 10 -> 10, of which waited for: 8 -> 8; matrix products, arithmetic and copies ran while one was open for 4% -> 5% of each run, Pallas kernels for 1% -> 3%
where the time goes in v4:
time: 91 us; the launch traced here: 90.3 us
  starting transfers between devices  45.7 us (50%)
  waiting for transfers between devices  24.3 us (27%)
  Pallas kernels  13 us (14%)
  other arithmetic  3.98 us (4%)
  local copies, waits for them, and re-layouts  2.61 us (3%)
    ppermute x6, starting transfers between devices, turned(): lax.ppermute(block, axis, [(i, (i + distance) % size) for i in range(size)])  25.8 us
    all_to_all x2, starting transfers between devices, crossed(): lax.all_to_all(flat, ('yhi', 'head'), split_axis=0, concat_axis=0, tiled=...  12.7 us
    ppermute x6, waiting for transfers between devices, turned(): lax.ppermute(block, axis, [(i, (i + distance) % size) for i in range(size)])  12.3 us
    all_to_all x2, waiting for transfers between devices, crossed(): lax.all_to_all(flat, ('yhi', 'head'), split_axis=0, concat_axis=0, tiled=...  10.1 us
    pallas_call x1, Pallas kernels, attention(): pl.pallas_call(attention_kernel, out_shape=(jax.ShapeDtypeStruct(moved.sh...  9.65 us
    all_to_all x2, starting transfers between devices, swapped(): lax.all_to_all(block, 'head', split_axis=0, concat_axis=0, tiled=True)  7.14 us
    all_to_all x2, waiting for transfers between devices, swapped(): lax.all_to_all(block, 'head', split_axis=0, concat_axis=0, tiled=True)  1.84 us
  transfers between devices with their start and end apart: 10, of which 8 were waited for; matrix products, arithmetic and copies ran while one was open for 5% of the time, Pallas kernels for 3%

profile of v4, /device:TPU:1, one launch (start us, length us, event | category | flops | bytes accessed | tf_op | source)
XLA Modules:
  0.0 90.3 jit_solution(9496696560450083758)
XLA Ops:
  0.6 0.8 maximum_bitcast_fusion
  1.4 0.7 broadcast_in_dim.2
  2.1 7.6 %all-to-all-start = ((bf16[16,2,16,128]{3,2,1,0:T(8,128)(2,1)}), bf16[16,2,16,128]{3,2,1,0:T(8,128)(2,1)S(1)}, u32[]{:S(2)}, u32[]{:S(2)}) async-start(bf16[16,2,16,128]{3,2,1,0:T(8,128)(2,1)} %bitcast.5), calls=%async_computation | async-start | bytes 262144 | tf_op jit(solution)/shard_map/all_to_all | solution.py:337
  9.7 1.3 %pad_maximum_fusion = bf16[2,16,128,128]{3,2,1,0:T(8,128)(2,1)S(1)} fusion(bf16[1,16,128,128]{3,2,1,0:T(8,128)(2,1)} %bitcast.41, bf16[1,16,128,128]{3,2,1,0:T(8,128)(2,1)} %bitcast.42), kind=kLoop, calls=%fused_computation | loop fusion | flops 524288 | bytes 2097152 | tf_op jit(solution)/shard_map/stack | solution.py:348
  11.0 1.2 %copy.13 = bf16[32,8,16,128]{3,2,0,1:T(8,128)(2,1)} copy(bf16[32,8,16,128]{3,2,1,0:T(8,128)(2,1)S(1)} %bitcast.37) | data formatting | bytes 2097152 | tf_op jit(solution)/shard_map/reshape | solution.py:348
  12.2 4.4 %all-to-all-done = bf16[16,2,16,128]{3,2,1,0:T(8,128)(2,1)S(1)} async-done(((bf16[16,2,16,128]{3,2,1,0:T(8,128)(2,1)}), bf16[16,2,16,128]{3,2,1,0:T(8,128)(2,1)S(1)}, u32[]{:S(2)}, u32[]{:S(2)}) %all-to-all-start) | async-done | bytes 131104 | tf_op jit(solution)/shard_map/all_to_all | solution.py:337
  16.5 4.9 %collective-permute-start.1 = (bf16[2,8,2,16,128]{4,3,2,1,0:T(8,128)(2,1)S(1)}, bf16[2,8,2,16,128]{4,3,2,1,0:T(8,128)(2,1)S(1)}, u32[]{:S(2)}, u32[]{:S(2)}) collective-permute-start(bf16[2,8,2,16,128]{4,3,2,1,0:T(8,128)(2,1)S(1)} %bitcast.38), channel_id=1, source_target_pairs={{0,64},{32,96},{64,128},{96,160},{128,192},{160,224},{192,256},{22... | collective-permute-start | bytes 393224 | tf_op jit(solution)/shard_map/ppermute | solution.py:328
  21.5 3.5 %collective-permute-start = (bf16[2,8,2,16,128]{4,3,2,1,0:T(8,128)(2,1)S(1)}, bf16[2,8,2,16,128]{4,3,2,1,0:T(8,128)(2,1)S(1)}, u32[]{:S(2)}, u32[]{:S(2)}) collective-permute-start(bf16[2,8,2,16,128]{4,3,2,1,0:T(8,128)(2,1)S(1)} %bitcast.39), channel_id=1, source_target_pairs={{0,32},{32,64},{64,96},{96,128},{128,160},{160,192},{192,224},{224... | collective-permute-start | bytes 393224 | tf_op jit(solution)/shard_map/ppermute | solution.py:328
  25.0 3.6 %all-to-all-start.1 = ((bf16[8,32,16,128]{3,2,1,0:T(8,128)(2,1)}), bf16[8,32,16,128]{3,2,1,0:T(8,128)(2,1)S(1)}, u32[]{:S(2)}, u32[]{:S(2)}) async-start(bf16[8,32,16,128]{3,2,1,0:T(8,128)(2,1)} %bitcast.35), calls=%async_computation.1 | async-start | bytes 2097152 | tf_op jit(solution)/shard_map/all_to_all | solution.py:332
  28.6 0.0 copy-start
  28.6 2.0 %collective-permute-done.1.block = bf16[2,8,2,16,128]{4,3,2,1,0:T(8,128)(2,1)S(1)} collective-permute-done((bf16[2,8,2,16,128]{4,3,2,1,0:T(8,128)(2,1)S(1)}, bf16[2,8,2,16,128]{4,3,2,1,0:T(8,128)(2,1)S(1)}, u32[]{:S(2)}, u32[]{:S(2)}) %collective-permute-start.1) | collective-permute-done | bytes 131104 | tf_op jit(solution)/shard_map/ppermute | solution.py:328
  30.6 0.0 copy-start.1
  30.6 0.7 copy-done.1
  31.2 1.6 %held.1 = bf16[2,8,2,16,128]{4,3,2,1,0:T(8,128)(2,1)} custom-call(bf16[2,8,2,16,128]{4,3,2,1,0:T(8,128)(2,1)} %copy-done.1), custom_call_target="tpu_custom_call" | custom-call | flops 5000000000 | bytes 262144 | tf_op jit(solution)/shard_map/held/pallas_call | solution.py:314
  32.8 3.6 %collective-permute-done = bf16[2,8,2,16,128]{4,3,2,1,0:T(8,128)(2,1)S(1)} collective-permute-done((bf16[2,8,2,16,128]{4,3,2,1,0:T(8,128)(2,1)S(1)}, bf16[2,8,2,16,128]{4,3,2,1,0:T(8,128)(2,1)S(1)}, u32[]{:S(2)}, u32[]{:S(2)}) %collective-permute-start) | collective-permute-done | bytes 131104 | tf_op jit(solution)/shard_map/ppermute | solution.py:328
  36.4 0.9 %pad_maximum_fusion.1.same_core = bf16[3,2,8,2,16,128]{5,4,3,2,1,0:T(8,128)(2,1)S(1)} fusion(bf16[1,2,8,2,16,128]{5,4,3,2,1,0:T(8,128)(2,1)} %bitcast.44, bf16[1,2,8,2,16,128]{5,4,3,2,1,0:T(8,128)(2,1)S(1)} %bitcast.43, bf16[1,2,8,2,16,128]{5,4,3,2,1,0:T(8,128)(2,1)S(1)} %bitcast.40), kind=kLoop, calls=%fused_computation.5 | loop fusion | flops 393216 | bytes 786432 | tf_op jit(solution)/shard_map/stack | solution.py:354
  37.4 3.8 %collective-permute-start.2 = (bf16[3,2,8,2,16,128]{5,4,3,2,1,0:T(8,128)(2,1)S(1)}, bf16[3,2,8,2,16,128]{5,4,3,2,1,0:T(8,128)(2,1)S(1)}, u32[]{:S(2)}, u32[]{:S(2)}) collective-permute-start(bf16[3,2,8,2,16,128]{5,4,3,2,1,0:T(8,128)(2,1)S(1)} %pad_maximum_fusion.1.same_core), channel_id=1, source_target_pairs={{0,8},{8,0},{1,9},{9,1},{2,10},{10,2},{3,11},{11,3},{4,12},{12,4},... | collective-permute-start | bytes 1179656 | tf_op jit(solution)/shard_map/ppermute | solution.py:328
  41.2 0.1 pad_add_fusion.places
  41.2 1.2 %collective-permute-done.2.other_core = bf16[3,2,8,2,16,128]{5,4,3,2,1,0:T(8,128)(2,1)S(1)} collective-permute-done((bf16[3,2,8,2,16,128]{5,4,3,2,1,0:T(8,128)(2,1)S(1)}, bf16[3,2,8,2,16,128]{5,4,3,2,1,0:T(8,128)(2,1)S(1)}, u32[]{:S(2)}, u32[]{:S(2)}) %collective-permute-start.2) | collective-permute-done | bytes 393248 | tf_op jit(solution)/shard_map/ppermute | solution.py:328
  42.5 1.8 %all-to-all-done.1.moved = bf16[8,32,16,128]{3,2,1,0:T(8,128)(2,1)S(1)} async-done(((bf16[8,32,16,128]{3,2,1,0:T(8,128)(2,1)}), bf16[8,32,16,128]{3,2,1,0:T(8,128)(2,1)S(1)}, u32[]{:S(2)}, u32[]{:S(2)}) %all-to-all-start.1) | async-done | bytes 1048608 | tf_op jit(solution)/shard_map/all_to_all | solution.py:332
  44.3 0.0 copy-done
  44.3 9.6 %attention.1 = (bf16[8,32,16,128]{3,2,1,0:T(8,128)(2,1)}, f32[2,3,2,8,2,16,128]{6,5,4,3,2,1,0:T(8,128)S(1)}) custom-call(s32[2]{0:T(128)S(1)} %pad_add_fusion.places, s32[16]{0:T(128)S(1)} %copy-done, bf16[8,32,16,128]{3,2,1,0:T(8,128)(2,1)S(1)} %all-to-all-done.1.moved, bf16[3,2,8,2,16,128]{5,4,3,2,1,0:T(8,128)(2,1)S(1)} %pad_maximum_fusion.1.same_core, ...), custom_call_target="tpu_custom_call" | custom-call | flops 3623878656 | bytes 2883584 | tf_op jit(solution)/shard_map/attention/pallas_call | solution.py:223
  54.0 0.1 fusion
  54.1 2.8 %collective-permute-start.3 = (bf16[3,2,8,2,16,128]{5,4,3,2,1,0:T(8,128)(2,1)S(1)}, bf16[3,2,8,2,16,128]{5,4,3,2,1,0:T(8,128)(2,1)S(1)}, u32[]{:S(2)}, u32[]{:S(2)}) collective-permute-start(bf16[3,2,8,2,16,128]{5,4,3,2,1,0:T(8,128)(2,1)S(1)} %fusion), channel_id=1, source_target_pairs={{0,8},{8,0},{1,9},{9,1},{2,10},{10,2},{3,11},{11,3},{4,12},{12,4},... | collective-permute-start | bytes 1179656 | tf_op jit(solution)/shard_map/ppermute | solution.py:328
  56.8 3.6 %all-to-all-start.2 = ((bf16[8,32,16,128]{3,2,1,0:T(8,128)(2,1)}), bf16[8,32,16,128]{3,2,1,0:T(8,128)(2,1)S(1)}, u32[]{:S(2)}, u32[]{:S(2)}) async-start(bf16[8,32,16,128]{3,2,1,0:T(8,128)(2,1)} %get-tuple-element.16), calls=%async_computation.2 | async-start | bytes 2097152 | tf_op jit(solution)/shard_map/all_to_all | solution.py:332
  60.4 0.0 collective-permute-done.3
  60.4 0.2 fusion.4
  60.6 7.7 %collective-permute-start.4 = (bf16[2,8,2,16,128]{4,3,2,1,0:T(8,128)(2,1)S(1)}, bf16[2,8,2,16,128]{4,3,2,1,0:T(8,128)(2,1)S(1)}, u32[]{:S(2)}, u32[]{:S(2)}) collective-permute-start(bf16[2,8,2,16,128]{4,3,2,1,0:T(8,128)(2,1)S(1)} %get-tuple-element.26), channel_id=1, source_target_pairs={{0,448},{32,480},{64,0},{96,32},{128,64},{160,96},{192,128},{224,1... | collective-permute-start | bytes 393224 | tf_op jit(solution)/shard_map/ppermute | solution.py:328
  68.3 3.1 %collective-permute-start.5 = (bf16[2,8,2,16,128]{4,3,2,1,0:T(8,128)(2,1)S(1)}, bf16[2,8,2,16,128]{4,3,2,1,0:T(8,128)(2,1)S(1)}, u32[]{:S(2)}, u32[]{:S(2)}) collective-permute-start(bf16[2,8,2,16,128]{4,3,2,1,0:T(8,128)(2,1)S(1)} %get-tuple-element.27), channel_id=1, source_target_pairs={{0,480},{32,0},{64,32},{96,64},{128,96},{160,128},{192,160},{224,1... | collective-permute-start | bytes 393224 | tf_op jit(solution)/shard_map/ppermute | solution.py:328
  71.4 2.5 %collective-permute-done.4 = bf16[2,8,2,16,128]{4,3,2,1,0:T(8,128)(2,1)S(1)} collective-permute-done((bf16[2,8,2,16,128]{4,3,2,1,0:T(8,128)(2,1)S(1)}, bf16[2,8,2,16,128]{4,3,2,1,0:T(8,128)(2,1)S(1)}, u32[]{:S(2)}, u32[]{:S(2)}) %collective-permute-start.4) | collective-permute-done | bytes 131104 | tf_op jit(solution)/shard_map/ppermute | solution.py:328
  74.0 3.0 %collective-permute-done.5 = bf16[2,8,2,16,128]{4,3,2,1,0:T(8,128)(2,1)S(1)} collective-permute-done((bf16[2,8,2,16,128]{4,3,2,1,0:T(8,128)(2,1)S(1)}, bf16[2,8,2,16,128]{4,3,2,1,0:T(8,128)(2,1)S(1)}, u32[]{:S(2)}, u32[]{:S(2)}) %collective-permute-start.5) | collective-permute-done | bytes 131104 | tf_op jit(solution)/shard_map/ppermute | solution.py:328
  76.9 0.7 fusion.3
  77.6 0.0 all-to-all-done.2.back
  77.6 5.1 %all-to-all-start.3 = ((bf16[16,2,16,128]{3,2,1,0:T(8,128)(2,1)}), bf16[16,2,16,128]{3,2,1,0:T(8,128)(2,1)S(1)}, u32[]{:S(2)}, u32[]{:S(2)}) async-start(bf16[16,2,16,128]{3,2,1,0:T(8,128)(2,1)} %bitcast.19), calls=%async_computation.3 | async-start | bytes 262144 | tf_op jit(solution)/shard_map/all_to_all | solution.py:337
  82.8 1.1 %spread.1 = (bf16[16,128,128]{2,1,0:T(8,128)(2,1)}, bf16[16,128,128]{2,1,0:T(8,128)(2,1)}) custom-call(bf16[8,32,16,128]{3,2,1,0:T(8,128)(2,1)S(1)} %all-to-all-done.2.back), custom_call_target="tpu_custom_call" | custom-call | tf_op jit(solution)/shard_map/spread/pallas_call | solution.py:275
  83.9 5.7 %all-to-all-done.3 = bf16[16,2,16,128]{3,2,1,0:T(8,128)(2,1)S(1)} async-done(((bf16[16,2,16,128]{3,2,1,0:T(8,128)(2,1)}), bf16[16,2,16,128]{3,2,1,0:T(8,128)(2,1)S(1)}, u32[]{:S(2)}, u32[]{:S(2)}) %all-to-all-start.3) | async-done | bytes 131104 | tf_op jit(solution)/shard_map/all_to_all | solution.py:337
  89.6 0.7 split.1
  (2 shorter events, 0.0 us)
Async XLA Ops:
  2.1 14.4 %all-to-all-start = ((bf16[16,2,16,128]{3,2,1,0:T(8,128)(2,1)}), bf16[16,2,16,128]{3,2,1,0:T(8,128)(2,1)S(1)}, u32[]{:S(2)}, u32[]{:S(2)}) async-start(bf16[16,2,16,128]{3,2,1,0:T(8,128)(2,1)} %bitcast.5), calls=%async_computation | async-start | bytes 262144 | tf_op jit(solution)/shard_map/all_to_all | solution.py:337
  16.5 14.0 %collective-permute-start.1 = (bf16[2,8,2,16,128]{4,3,2,1,0:T(8,128)(2,1)S(1)}, bf16[2,8,2,16,128]{4,3,2,1,0:T(8,128)(2,1)S(1)}, u32[]{:S(2)}, u32[]{:S(2)}) collective-permute-start(bf16[2,8,2,16,128]{4,3,2,1,0:T(8,128)(2,1)S(1)} %bitcast.38), channel_id=1, source_target_pairs={{0,64},{32,96},{64,128},{96,160},{128,192},{160,224},{192,256},{22... | collective-permute-start | bytes 393224 | tf_op jit(solution)/shard_map/ppermute | solution.py:328
  21.5 15.0 %collective-permute-start = (bf16[2,8,2,16,128]{4,3,2,1,0:T(8,128)(2,1)S(1)}, bf16[2,8,2,16,128]{4,3,2,1,0:T(8,128)(2,1)S(1)}, u32[]{:S(2)}, u32[]{:S(2)}) collective-permute-start(bf16[2,8,2,16,128]{4,3,2,1,0:T(8,128)(2,1)S(1)} %bitcast.39), channel_id=1, source_target_pairs={{0,32},{32,64},{64,96},{96,128},{128,160},{160,192},{192,224},{224... | collective-permute-start | bytes 393224 | tf_op jit(solution)/shard_map/ppermute | solution.py:328
  25.0 19.3 %all-to-all-start.1 = ((bf16[8,32,16,128]{3,2,1,0:T(8,128)(2,1)}), bf16[8,32,16,128]{3,2,1,0:T(8,128)(2,1)S(1)}, u32[]{:S(2)}, u32[]{:S(2)}) async-start(bf16[8,32,16,128]{3,2,1,0:T(8,128)(2,1)} %bitcast.35), calls=%async_computation.1 | async-start | bytes 2097152 | tf_op jit(solution)/shard_map/all_to_all | solution.py:332
  28.6 15.7 %copy-start = (s32[16]{0:T(128)S(1)}, s32[16]{0:T(128)}, u32[]{:S(2)}) copy-start(s32[16]{0:T(128)} %lengths.1) | copy-start | bytes 196
  30.6 0.7 copy-start.1
  37.4 5.1 %collective-permute-start.2 = (bf16[3,2,8,2,16,128]{5,4,3,2,1,0:T(8,128)(2,1)S(1)}, bf16[3,2,8,2,16,128]{5,4,3,2,1,0:T(8,128)(2,1)S(1)}, u32[]{:S(2)}, u32[]{:S(2)}) collective-permute-start(bf16[3,2,8,2,16,128]{5,4,3,2,1,0:T(8,128)(2,1)S(1)} %pad_maximum_fusion.1.same_core), channel_id=1, source_target_pairs={{0,8},{8,0},{1,9},{9,1},{2,10},{10,2},{3,11},{11,3},{4,12},{12,4},... | collective-permute-start | bytes 1179656 | tf_op jit(solution)/shard_map/ppermute | solution.py:328
  54.1 6.3 %collective-permute-start.3 = (bf16[3,2,8,2,16,128]{5,4,3,2,1,0:T(8,128)(2,1)S(1)}, bf16[3,2,8,2,16,128]{5,4,3,2,1,0:T(8,128)(2,1)S(1)}, u32[]{:S(2)}, u32[]{:S(2)}) collective-permute-start(bf16[3,2,8,2,16,128]{5,4,3,2,1,0:T(8,128)(2,1)S(1)} %fusion), channel_id=1, source_target_pairs={{0,8},{8,0},{1,9},{9,1},{2,10},{10,2},{3,11},{11,3},{4,12},{12,4},... | collective-permute-start | bytes 1179656 | tf_op jit(solution)/shard_map/ppermute | solution.py:328
  56.8 20.8 %all-to-all-start.2 = ((bf16[8,32,16,128]{3,2,1,0:T(8,128)(2,1)}), bf16[8,32,16,128]{3,2,1,0:T(8,128)(2,1)S(1)}, u32[]{:S(2)}, u32[]{:S(2)}) async-start(bf16[8,32,16,128]{3,2,1,0:T(8,128)(2,1)} %get-tuple-element.16), calls=%async_computation.2 | async-start | bytes 2097152 | tf_op jit(solution)/shard_map/all_to_all | solution.py:332
  60.6 13.4 %collective-permute-start.4 = (bf16[2,8,2,16,128]{4,3,2,1,0:T(8,128)(2,1)S(1)}, bf16[2,8,2,16,128]{4,3,2,1,0:T(8,128)(2,1)S(1)}, u32[]{:S(2)}, u32[]{:S(2)}) collective-permute-start(bf16[2,8,2,16,128]{4,3,2,1,0:T(8,128)(2,1)S(1)} %get-tuple-element.26), channel_id=1, source_target_pairs={{0,448},{32,480},{64,0},{96,32},{128,64},{160,96},{192,128},{224,1... | collective-permute-start | bytes 393224 | tf_op jit(solution)/shard_map/ppermute | solution.py:328
  68.3 8.6 %collective-permute-start.5 = (bf16[2,8,2,16,128]{4,3,2,1,0:T(8,128)(2,1)S(1)}, bf16[2,8,2,16,128]{4,3,2,1,0:T(8,128)(2,1)S(1)}, u32[]{:S(2)}, u32[]{:S(2)}) collective-permute-start(bf16[2,8,2,16,128]{4,3,2,1,0:T(8,128)(2,1)S(1)} %get-tuple-element.27), channel_id=1, source_target_pairs={{0,480},{32,0},{64,32},{96,64},{128,96},{160,128},{192,160},{224,1... | collective-permute-start | bytes 393224 | tf_op jit(solution)/shard_map/ppermute | solution.py:328
  77.6 12.0 %all-to-all-start.3 = ((bf16[16,2,16,128]{3,2,1,0:T(8,128)(2,1)}), bf16[16,2,16,128]{3,2,1,0:T(8,128)(2,1)S(1)}, u32[]{:S(2)}, u32[]{:S(2)}) async-start(bf16[16,2,16,128]{3,2,1,0:T(8,128)(2,1)} %bitcast.19), calls=%async_computation.3 | async-start | bytes 262144 | tf_op jit(solution)/shard_map/all_to_all | solution.py:337

commit v5 on v3

--- a/solution.py
+++ b/solution.py
@@ -86,17 +86,30 @@
         if after:
             held[pl.ds(span - after, after), lanes_of(chunk)] = jnp.zeros((after, rows), held.dtype)
 
+    def three_blocks(held, right, first, chunk):
+        low = first * block + live(first, chunk)[0]
+        high = (first + 2) * block + live(first + 2, chunk)[1]
+        result = dot(held[pl.ds(low, high - low), :], right, ((1,), (0,)))
+        pieces = {}
+        for index in range(first, first + 3):
+            start, stop = live(index, chunk)
+            pieces[index] = result[index * block + start - low : index * block + stop - low]
+        return pieces
+
     state = {}
 
     def leaving(chunk):
         return pltpu.make_async_copy(ready.at[chunk], out_moved.at[chunk], sems.at[chunk])
 
     def forward(chunk):
-        query, _ = operands(chunk)
+        query_t = operands(chunk)[0].T
         low = first_keys(chunk)
+        pieces = {}
         highest, total, seen = None, None, {}
-        for index in [REACH] + list(range(REACH)):
-            scores = dot(keys[rows_of(index, chunk), :], query, ((1,), (1,)))
+        for index in [REACH, REACH - 1, REACH - 2] + list(range(REACH - 2)):
+            if index not in pieces:
+                pieces = three_blocks(keys, query_t, index - index % 3, chunk)
+            scores = pieces[index]
             first, last = live(index, chunk)
             key_row = lax.broadcasted_iota(jnp.int32, (last - first, rows), 0) + first
             allowed = key_row >= low - index * block
@@ -124,7 +137,7 @@
         }
 
     def backward(chunk):
-        query, grad = operands(chunk)
+        grad_t = operands(chunk)[1].T
         factors = state.pop(chunk)
         for index in range(REACH + 1):
             part = rows_of(index, chunk)
@@ -135,13 +148,14 @@
         attended = attended.astype(jnp.bfloat16)
         ready[chunk, :chunk_tok] = attended.T.reshape(chunk_tok, group, width)
         delta = jnp.sum(
-            grad.T.astype(jnp.float32) * attended.astype(jnp.float32), axis=0, keepdims=True
+            grad_t.astype(jnp.float32) * attended.astype(jnp.float32), axis=0, keepdims=True
         )
         yield
         for index in range(REACH + 1):
             part = rows_of(index, chunk)
-            dprob = dot(values[part, :], grad, ((1,), (1,)))
-            slope = (dprob - delta).astype(jnp.bfloat16)
+            if index % 3 == 0:
+                pieces = three_blocks(values, grad_t, index, chunk)
+            slope = (pieces[index] - delta).astype(jnp.bfloat16)
             dscore_all[part, lanes_of(chunk)] = weight_all[part, lanes_of(chunk)] * slope
             yield
         clear(dscore_all, chunk)

time: 89.4 us -> 89.3 us (level)
  no operation moved by 1% of the time
where the time goes in v5:
time: 89.3 us; the launch traced here: 88.6 us
  starting transfers between devices  41.3 us (46%)
  waiting for transfers between devices  30.1 us (34%)
  Pallas kernels  11.4 us (13%)
  other arithmetic  3.08 us (3%)
  local copies, waits for them, and re-layouts  1.94 us (2%)
    ppermute x6, starting transfers between devices, turned(): lax.ppermute(block, axis, [(i, (i + distance) % size) for i in range(size)])  21.6 us
    ppermute x6, waiting for transfers between devices, turned(): lax.ppermute(block, axis, [(i, (i + distance) % size) for i in range(size)])  18.4 us
    all_to_all x2, starting transfers between devices, crossed(): lax.all_to_all(flat, ('yhi', 'head'), split_axis=0, concat_axis=0, tiled=...  11.1 us
    all_to_all x2, waiting for transfers between devices, crossed(): lax.all_to_all(flat, ('yhi', 'head'), split_axis=0, concat_axis=0, tiled=...  10.1 us
    pallas_call x1, Pallas kernels, attention(): pl.pallas_call(attention_kernel, out_shape=(jax.ShapeDtypeStruct(moved.sh...  9.59 us
    all_to_all x2, starting transfers between devices, swapped(): lax.all_to_all(block, 'head', split_axis=0, concat_axis=0, tiled=True)  8.63 us
  transfers between devices with their start and end apart: 10, of which 8 were waited for; matrix products, arithmetic and copies ran while one was open for 4% of the time, Pallas kernels for 1%

profile of v5, /device:TPU:1, one launch (start us, length us, event | category | flops | bytes accessed | tf_op | source)
XLA Modules:
  0.0 88.6 jit_solution(7522377336177675578)
XLA Ops:
  0.6 0.8 maximum_bitcast_fusion
  1.4 0.7 broadcast_in_dim.2
  2.1 7.6 %all-to-all-start = ((bf16[16,2,16,128]{3,2,1,0:T(8,128)(2,1)}), bf16[16,2,16,128]{3,2,1,0:T(8,128)(2,1)S(1)}, u32[]{:S(2)}, u32[]{:S(2)}) async-start(bf16[16,2,16,128]{3,2,1,0:T(8,128)(2,1)} %bitcast.5), calls=%async_computation | async-start | bytes 262144 | tf_op jit(solution)/shard_map/all_to_all | solution.py:333
  9.7 1.3 %pad_maximum_fusion = bf16[2,16,128,128]{3,2,1,0:T(8,128)(2,1)S(1)} fusion(bf16[1,16,128,128]{3,2,1,0:T(8,128)(2,1)} %bitcast.41, bf16[1,16,128,128]{3,2,1,0:T(8,128)(2,1)} %bitcast.42), kind=kLoop, calls=%fused_computation | loop fusion | flops 524288 | bytes 2097152 | tf_op jit(solution)/shard_map/stack | solution.py:344
  11.0 1.2 %copy.13 = bf16[32,8,16,128]{3,2,0,1:T(8,128)(2,1)} copy(bf16[32,8,16,128]{3,2,1,0:T(8,128)(2,1)S(1)} %bitcast.37) | data formatting | bytes 2097152 | tf_op jit(solution)/shard_map/reshape | solution.py:344
  12.2 0.0 copy-start
  12.2 4.4 %all-to-all-done = bf16[16,2,16,128]{3,2,1,0:T(8,128)(2,1)S(1)} async-done(((bf16[16,2,16,128]{3,2,1,0:T(8,128)(2,1)}), bf16[16,2,16,128]{3,2,1,0:T(8,128)(2,1)S(1)}, u32[]{:S(2)}, u32[]{:S(2)}) %all-to-all-start) | async-done | bytes 131104 | tf_op jit(solution)/shard_map/all_to_all | solution.py:333
  16.5 3.6 %all-to-all-start.1 = ((bf16[8,32,16,128]{3,2,1,0:T(8,128)(2,1)}), bf16[8,32,16,128]{3,2,1,0:T(8,128)(2,1)S(1)}, u32[]{:S(2)}, u32[]{:S(2)}) async-start(bf16[8,32,16,128]{3,2,1,0:T(8,128)(2,1)} %bitcast.35), calls=%async_computation.1 | async-start | bytes 2097152 | tf_op jit(solution)/shard_map/all_to_all | solution.py:328
  20.1 4.9 %collective-permute-start.1 = (bf16[2,8,2,16,128]{4,3,2,1,0:T(8,128)(2,1)S(1)}, bf16[2,8,2,16,128]{4,3,2,1,0:T(8,128)(2,1)S(1)}, u32[]{:S(2)}, u32[]{:S(2)}) collective-permute-start(bf16[2,8,2,16,128]{4,3,2,1,0:T(8,128)(2,1)S(1)} %bitcast.38), channel_id=1, source_target_pairs={{0,64},{32,96},{64,128},{96,160},{128,192},{160,224},{192,256},{22... | collective-permute-start | bytes 393224 | tf_op jit(solution)/shard_map/ppermute | solution.py:324
  25.0 3.5 %collective-permute-start = (bf16[2,8,2,16,128]{4,3,2,1,0:T(8,128)(2,1)S(1)}, bf16[2,8,2,16,128]{4,3,2,1,0:T(8,128)(2,1)S(1)}, u32[]{:S(2)}, u32[]{:S(2)}) collective-permute-start(bf16[2,8,2,16,128]{4,3,2,1,0:T(8,128)(2,1)S(1)} %bitcast.39), channel_id=1, source_target_pairs={{0,32},{32,64},{64,96},{96,128},{128,160},{160,192},{192,224},{224... | collective-permute-start | bytes 393224 | tf_op jit(solution)/shard_map/ppermute | solution.py:324
  28.6 5.6 %collective-permute-done.1 = bf16[2,8,2,16,128]{4,3,2,1,0:T(8,128)(2,1)S(1)} collective-permute-done((bf16[2,8,2,16,128]{4,3,2,1,0:T(8,128)(2,1)S(1)}, bf16[2,8,2,16,128]{4,3,2,1,0:T(8,128)(2,1)S(1)}, u32[]{:S(2)}, u32[]{:S(2)}) %collective-permute-start.1) | collective-permute-done | bytes 131104 | tf_op jit(solution)/shard_map/ppermute | solution.py:324
  34.1 5.9 %collective-permute-done = bf16[2,8,2,16,128]{4,3,2,1,0:T(8,128)(2,1)S(1)} collective-permute-done((bf16[2,8,2,16,128]{4,3,2,1,0:T(8,128)(2,1)S(1)}, bf16[2,8,2,16,128]{4,3,2,1,0:T(8,128)(2,1)S(1)}, u32[]{:S(2)}, u32[]{:S(2)}) %collective-permute-start) | collective-permute-done | bytes 131104 | tf_op jit(solution)/shard_map/ppermute | solution.py:324
  40.0 3.2 %collective-permute-start.2 = (bf16[3,2,8,2,16,128]{5,4,3,2,1,0:T(8,128)(2,1)S(1)}, bf16[3,2,8,2,16,128]{5,4,3,2,1,0:T(8,128)(2,1)S(1)}, u32[]{:S(2)}, u32[]{:S(2)}) collective-permute-start(bf16[3,2,8,2,16,128]{5,4,3,2,1,0:T(8,128)(2,1)S(1)} %pad_maximum_fusion.1.same_core), channel_id=1, source_target_pairs={{0,8},{8,0},{1,9},{9,1},{2,10},{10,2},{3,11},{11,3},{4,12},{12,4},... | collective-permute-start | bytes 1179656 | tf_op jit(solution)/shard_map/ppermute | solution.py:324
  43.3 0.1 pad_add_fusion.places
  43.4 1.2 %collective-permute-done.2.other_core = bf16[3,2,8,2,16,128]{5,4,3,2,1,0:T(8,128)(2,1)S(1)} collective-permute-done((bf16[3,2,8,2,16,128]{5,4,3,2,1,0:T(8,128)(2,1)S(1)}, bf16[3,2,8,2,16,128]{5,4,3,2,1,0:T(8,128)(2,1)S(1)}, u32[]{:S(2)}, u32[]{:S(2)}) %collective-permute-start.2) | collective-permute-done | bytes 393248 | tf_op jit(solution)/shard_map/ppermute | solution.py:324
  44.6 0.0 all-to-all-done.1.moved
  44.6 0.0 copy-done
  44.6 9.6 %attention.1 = (bf16[8,32,16,128]{3,2,1,0:T(8,128)(2,1)}, f32[2,3,2,8,2,16,128]{6,5,4,3,2,1,0:T(8,128)S(1)}) custom-call(s32[2]{0:T(128)S(1)} %pad_add_fusion.places, s32[16]{0:T(128)S(1)} %copy-done, bf16[8,32,16,128]{3,2,1,0:T(8,128)(2,1)S(1)} %all-to-all-done.1.moved, bf16[3,2,8,2,16,128]{5,4,3,2,1,0:T(8,128)(2,1)S(1)} %pad_maximum_fusion.1.same_core, ...), custom_call_target="tpu_custom_call" | custom-call | flops 3623878656 | bytes 2883584 | tf_op jit(solution)/shard_map/attention/pallas_call | solution.py:237
  54.2 0.1 fusion
  54.3 2.3 %collective-permute-start.3 = (bf16[3,2,8,2,16,128]{5,4,3,2,1,0:T(8,128)(2,1)S(1)}, bf16[3,2,8,2,16,128]{5,4,3,2,1,0:T(8,128)(2,1)S(1)}, u32[]{:S(2)}, u32[]{:S(2)}) collective-permute-start(bf16[3,2,8,2,16,128]{5,4,3,2,1,0:T(8,128)(2,1)S(1)} %fusion), channel_id=1, source_target_pairs={{0,8},{8,0},{1,9},{9,1},{2,10},{10,2},{3,11},{11,3},{4,12},{12,4},... | collective-permute-start | bytes 1179656 | tf_op jit(solution)/shard_map/ppermute | solution.py:324
  56.6 5.1 %all-to-all-start.2 = ((bf16[8,32,16,128]{3,2,1,0:T(8,128)(2,1)}), bf16[8,32,16,128]{3,2,1,0:T(8,128)(2,1)S(1)}, u32[]{:S(2)}, u32[]{:S(2)}) async-start(bf16[8,32,16,128]{3,2,1,0:T(8,128)(2,1)} %get-tuple-element.16), calls=%async_computation.2 | async-start | bytes 2097152 | tf_op jit(solution)/shard_map/all_to_all | solution.py:328
  61.6 0.0 collective-permute-done.3
  61.6 0.2 fusion.4
  61.8 4.3 %collective-permute-start.4 = (bf16[2,8,2,16,128]{4,3,2,1,0:T(8,128)(2,1)S(1)}, bf16[2,8,2,16,128]{4,3,2,1,0:T(8,128)(2,1)S(1)}, u32[]{:S(2)}, u32[]{:S(2)}) collective-permute-start(bf16[2,8,2,16,128]{4,3,2,1,0:T(8,128)(2,1)S(1)} %get-tuple-element.26), channel_id=1, source_target_pairs={{0,448},{32,480},{64,0},{96,32},{128,64},{160,96},{192,128},{224,1... | collective-permute-start | bytes 393224 | tf_op jit(solution)/shard_map/ppermute | solution.py:324
  66.1 3.3 %collective-permute-start.5 = (bf16[2,8,2,16,128]{4,3,2,1,0:T(8,128)(2,1)S(1)}, bf16[2,8,2,16,128]{4,3,2,1,0:T(8,128)(2,1)S(1)}, u32[]{:S(2)}, u32[]{:S(2)}) collective-permute-start(bf16[2,8,2,16,128]{4,3,2,1,0:T(8,128)(2,1)S(1)} %get-tuple-element.27), channel_id=1, source_target_pairs={{0,480},{32,0},{64,32},{96,64},{128,96},{160,128},{192,160},{224,1... | collective-permute-start | bytes 393224 | tf_op jit(solution)/shard_map/ppermute | solution.py:324
  69.5 2.7 %collective-permute-done.4 = bf16[2,8,2,16,128]{4,3,2,1,0:T(8,128)(2,1)S(1)} collective-permute-done((bf16[2,8,2,16,128]{4,3,2,1,0:T(8,128)(2,1)S(1)}, bf16[2,8,2,16,128]{4,3,2,1,0:T(8,128)(2,1)S(1)}, u32[]{:S(2)}, u32[]{:S(2)}) %collective-permute-start.4) | collective-permute-done | bytes 131104 | tf_op jit(solution)/shard_map/ppermute | solution.py:324
  72.2 3.0 %collective-permute-done.5 = bf16[2,8,2,16,128]{4,3,2,1,0:T(8,128)(2,1)S(1)} collective-permute-done((bf16[2,8,2,16,128]{4,3,2,1,0:T(8,128)(2,1)S(1)}, bf16[2,8,2,16,128]{4,3,2,1,0:T(8,128)(2,1)S(1)}, u32[]{:S(2)}, u32[]{:S(2)}) %collective-permute-start.5) | collective-permute-done | bytes 131104 | tf_op jit(solution)/shard_map/ppermute | solution.py:324
  75.2 0.7 fusion.3
  75.9 1.6 %all-to-all-done.2.back = bf16[8,32,16,128]{3,2,1,0:T(8,128)(2,1)S(1)} async-done(((bf16[8,32,16,128]{3,2,1,0:T(8,128)(2,1)}), bf16[8,32,16,128]{3,2,1,0:T(8,128)(2,1)S(1)}, u32[]{:S(2)}, u32[]{:S(2)}) %all-to-all-start.2) | async-done | bytes 1048608 | tf_op jit(solution)/shard_map/all_to_all | solution.py:328
  77.5 3.5 %all-to-all-start.3 = ((bf16[16,2,16,128]{3,2,1,0:T(8,128)(2,1)}), bf16[16,2,16,128]{3,2,1,0:T(8,128)(2,1)S(1)}, u32[]{:S(2)}, u32[]{:S(2)}) async-start(bf16[16,2,16,128]{3,2,1,0:T(8,128)(2,1)} %bitcast.19), calls=%async_computation.3 | async-start | bytes 262144 | tf_op jit(solution)/shard_map/all_to_all | solution.py:333
  81.0 1.1 %spread.1 = (bf16[16,128,128]{2,1,0:T(8,128)(2,1)}, bf16[16,128,128]{2,1,0:T(8,128)(2,1)}) custom-call(bf16[8,32,16,128]{3,2,1,0:T(8,128)(2,1)S(1)} %all-to-all-done.2.back), custom_call_target="tpu_custom_call" | custom-call | tf_op jit(solution)/shard_map/spread/pallas_call | solution.py:289
  82.1 5.7 %all-to-all-done.3 = bf16[16,2,16,128]{3,2,1,0:T(8,128)(2,1)S(1)} async-done(((bf16[16,2,16,128]{3,2,1,0:T(8,128)(2,1)}), bf16[16,2,16,128]{3,2,1,0:T(8,128)(2,1)S(1)}, u32[]{:S(2)}, u32[]{:S(2)}) %all-to-all-start.3) | async-done | bytes 131104 | tf_op jit(solution)/shard_map/all_to_all | solution.py:333
  87.9 0.7 split.1
  (3 shorter events, 0.1 us)
Async XLA Ops:
  2.1 14.4 %all-to-all-start = ((bf16[16,2,16,128]{3,2,1,0:T(8,128)(2,1)}), bf16[16,2,16,128]{3,2,1,0:T(8,128)(2,1)S(1)}, u32[]{:S(2)}, u32[]{:S(2)}) async-start(bf16[16,2,16,128]{3,2,1,0:T(8,128)(2,1)} %bitcast.5), calls=%async_computation | async-start | bytes 262144 | tf_op jit(solution)/shard_map/all_to_all | solution.py:333
  12.2 32.4 %copy-start = (s32[16]{0:T(128)S(1)}, s32[16]{0:T(128)}, u32[]{:S(2)}) copy-start(s32[16]{0:T(128)} %lengths.1) | copy-start | bytes 196
  16.5 28.1 %all-to-all-start.1 = ((bf16[8,32,16,128]{3,2,1,0:T(8,128)(2,1)}), bf16[8,32,16,128]{3,2,1,0:T(8,128)(2,1)S(1)}, u32[]{:S(2)}, u32[]{:S(2)}) async-start(bf16[8,32,16,128]{3,2,1,0:T(8,128)(2,1)} %bitcast.35), calls=%async_computation.1 | async-start | bytes 2097152 | tf_op jit(solution)/shard_map/all_to_all | solution.py:328
  20.1 14.0 %collective-permute-start.1 = (bf16[2,8,2,16,128]{4,3,2,1,0:T(8,128)(2,1)S(1)}, bf16[2,8,2,16,128]{4,3,2,1,0:T(8,128)(2,1)S(1)}, u32[]{:S(2)}, u32[]{:S(2)}) collective-permute-start(bf16[2,8,2,16,128]{4,3,2,1,0:T(8,128)(2,1)S(1)} %bitcast.38), channel_id=1, source_target_pairs={{0,64},{32,96},{64,128},{96,160},{128,192},{160,224},{192,256},{22... | collective-permute-start | bytes 393224 | tf_op jit(solution)/shard_map/ppermute | solution.py:324
  25.0 15.0 %collective-permute-start = (bf16[2,8,2,16,128]{4,3,2,1,0:T(8,128)(2,1)S(1)}, bf16[2,8,2,16,128]{4,3,2,1,0:T(8,128)(2,1)S(1)}, u32[]{:S(2)}, u32[]{:S(2)}) collective-permute-start(bf16[2,8,2,16,128]{4,3,2,1,0:T(8,128)(2,1)S(1)} %bitcast.39), channel_id=1, source_target_pairs={{0,32},{32,64},{64,96},{96,128},{128,160},{160,192},{192,224},{224... | collective-permute-start | bytes 393224 | tf_op jit(solution)/shard_map/ppermute | solution.py:324
  40.0 4.6 %collective-permute-start.2 = (bf16[3,2,8,2,16,128]{5,4,3,2,1,0:T(8,128)(2,1)S(1)}, bf16[3,2,8,2,16,128]{5,4,3,2,1,0:T(8,128)(2,1)S(1)}, u32[]{:S(2)}, u32[]{:S(2)}) collective-permute-start(bf16[3,2,8,2,16,128]{5,4,3,2,1,0:T(8,128)(2,1)S(1)} %pad_maximum_fusion.1.same_core), channel_id=1, source_target_pairs={{0,8},{8,0},{1,9},{9,1},{2,10},{10,2},{3,11},{11,3},{4,12},{12,4},... | collective-permute-start | bytes 1179656 | tf_op jit(solution)/shard_map/ppermute | solution.py:324
  54.3 7.4 %collective-permute-start.3 = (bf16[3,2,8,2,16,128]{5,4,3,2,1,0:T(8,128)(2,1)S(1)}, bf16[3,2,8,2,16,128]{5,4,3,2,1,0:T(8,128)(2,1)S(1)}, u32[]{:S(2)}, u32[]{:S(2)}) collective-permute-start(bf16[3,2,8,2,16,128]{5,4,3,2,1,0:T(8,128)(2,1)S(1)} %fusion), channel_id=1, source_target_pairs={{0,8},{8,0},{1,9},{9,1},{2,10},{10,2},{3,11},{11,3},{4,12},{12,4},... | collective-permute-start | bytes 1179656 | tf_op jit(solution)/shard_map/ppermute | solution.py:324
  56.6 21.0 %all-to-all-start.2 = ((bf16[8,32,16,128]{3,2,1,0:T(8,128)(2,1)}), bf16[8,32,16,128]{3,2,1,0:T(8,128)(2,1)S(1)}, u32[]{:S(2)}, u32[]{:S(2)}) async-start(bf16[8,32,16,128]{3,2,1,0:T(8,128)(2,1)} %get-tuple-element.16), calls=%async_computation.2 | async-start | bytes 2097152 | tf_op jit(solution)/shard_map/all_to_all | solution.py:328
  61.8 10.3 %collective-permute-start.4 = (bf16[2,8,2,16,128]{4,3,2,1,0:T(8,128)(2,1)S(1)}, bf16[2,8,2,16,128]{4,3,2,1,0:T(8,128)(2,1)S(1)}, u32[]{:S(2)}, u32[]{:S(2)}) collective-permute-start(bf16[2,8,2,16,128]{4,3,2,1,0:T(8,128)(2,1)S(1)} %get-tuple-element.26), channel_id=1, source_target_pairs={{0,448},{32,480},{64,0},{96,32},{128,64},{160,96},{192,128},{224,1... | collective-permute-start | bytes 393224 | tf_op jit(solution)/shard_map/ppermute | solution.py:324
  66.1 9.1 %collective-permute-start.5 = (bf16[2,8,2,16,128]{4,3,2,1,0:T(8,128)(2,1)S(1)}, bf16[2,8,2,16,128]{4,3,2,1,0:T(8,128)(2,1)S(1)}, u32[]{:S(2)}, u32[]{:S(2)}) collective-permute-start(bf16[2,8,2,16,128]{4,3,2,1,0:T(8,128)(2,1)S(1)} %get-tuple-element.27), channel_id=1, source_target_pairs={{0,480},{32,0},{64,32},{96,64},{128,96},{160,128},{192,160},{224,1... | collective-permute-start | bytes 393224 | tf_op jit(solution)/shard_map/ppermute | solution.py:324
  77.5 10.3 %all-to-all-start.3 = ((bf16[16,2,16,128]{3,2,1,0:T(8,128)(2,1)}), bf16[16,2,16,128]{3,2,1,0:T(8,128)(2,1)S(1)}, u32[]{:S(2)}, u32[]{:S(2)}) async-start(bf16[16,2,16,128]{3,2,1,0:T(8,128)(2,1)} %bitcast.19), calls=%async_computation.3 | async-start | bytes 262144 | tf_op jit(solution)/shard_map/all_to_all | solution.py:333
